TPU v7x, 768 devices: a whole 4x8x12 slice. The times are simulated.
768 devices in a mesh: fsdp: 64 (over y, x, core), dp: 12 (over z).
Axes of the slice: x: 4, y: 8, z: 12, core: 2. Of those that a mesh axis runs over, the one named last changes fastest.
Arguments:
- grads: bfloat16 [12, 4096, 14336], P('dp', 'fsdp')
- q_prev: float32 [32, 14336], replicated, may hold values from -6 to 6
Outputs:
- q_new: float32 [32, 14336], replicated
- resid_new: bfloat16 [12, 4096, 14336], P('dp', 'fsdp')
All inputs are finite; a program needn't handle non-finite values.
Results may differ from a plain program's by a relative error of at most 0.001.
Values sent between devices are 32-bit elements; how exact they have to be, the bound alone decides.
No kernel may reach another device: no remote copies, remote signals or barrier semaphores. Data moves between devices by JAX's collectives and lax.ppermute only.
A program may use at most 64 MiB of HBM per device.

v0:
```python
import jax
import jax.numpy as jnp
from jax import lax
from jax.sharding import PartitionSpec as P

HIGH = lax.Precision.HIGHEST


def per_device(grads, q_prev):
    corrected = grads[0].astype(jnp.float32)
    rank_width = q_prev.shape[0]
    local_left = lax.dot_general(
        corrected,
        q_prev,
        (((1,), (1,)), ((), ())),
        precision=HIGH,
        preferred_element_type=jnp.float32,
    )
    left = lax.psum(local_left, "dp")
    block_width = rank_width // 4
    basis = jnp.zeros_like(left)
    for block in range(4):
        columns = left[:, block * block_width : (block + 1) * block_width]
        if block > 0:
            coeffs = lax.psum(
                jnp.dot(basis.T, columns, precision=HIGH, preferred_element_type=jnp.float32),
                "fsdp",
            )
            columns = columns - jnp.dot(
                basis, coeffs, precision=HIGH, preferred_element_type=jnp.float32
            )
        block_gram = lax.psum(
            jnp.dot(columns.T, columns, precision=HIGH, preferred_element_type=jnp.float32), "fsdp"
        )
        block_lower = jnp.linalg.cholesky(block_gram)
        finished = lax.linalg.triangular_solve(
            block_lower, columns, left_side=False, lower=True, transpose_a=True
        )
        basis = lax.dynamic_update_slice_in_dim(basis, finished, block * block_width, 1)
    groups = lax.axis_size("dp")
    term = lax.dot_general(
        basis,
        corrected,
        (((0,), (0,)), ((), ())),
        precision=HIGH,
        preferred_element_type=jnp.float32,
    )
    q_new = lax.psum(term, ("fsdp", "dp")) / groups
    approx = jnp.dot(basis, q_new, precision=HIGH, preferred_element_type=jnp.float32)
    resid_new = (corrected - approx).astype(jnp.bfloat16)
    return (q_new, resid_new[None])


def solution(mesh):
    in_specs = (P("dp", "fsdp", None), P())
    out_specs = (P(), P("dp", "fsdp", None))
    return jax.shard_map(
        per_device, mesh=mesh, in_specs=in_specs, out_specs=out_specs, check_vma=False
    )
```

profile of v0, /device:TPU:1, one launch (start us, length us, event | category | flops | bytes accessed | tf_op | source)
XLA Modules:
  0.0 1795.8 jit_solution(8044237933199521712)
XLA Ops:
  7.2 1.4 copy-done
  8.7 3.0 fusion.4
  11.7 42.8 %psum.63 = f32[64,32]{0,1:T(8,128)S(1)} all-reduce(f32[64,32]{0,1:T(8,128)S(1)} %fusion.4), channel_id=1, replica_groups=mesh['fsdp'=64,'dp'=12] {'dp'}, use_global_device_ids=true, to_apply=%region_0.0 | all-reduce | flops 2048 | bytes 16384 | tf_op jit(solution)/shard_map/psum | solution.py:19
  54.6 135.3 %psum.64 = f32[8,8]{0,1:T(8,128)S(1)} all-reduce(f32[8,8]{0,1:T(8,128)S(1)} %fusion.30), channel_id=1, replica_groups=mesh['fsdp'=64,'dp'=12] {'fsdp'}, use_global_device_ids=true, to_apply=%region_1.0 | all-reduce | flops 64 | bytes 512 | tf_op jit(solution)/shard_map/psum | solution.py:32
  189.9 0.7 cholesky.74
  191.3 0.6 fusion.12
  193.0 241.0 %psum.65 = f32[32,8]{1,0:T(8,128)S(1)} all-reduce(f32[32,8]{1,0:T(8,128)S(1)} %fusion.10), channel_id=1, replica_groups=mesh['fsdp'=64,'dp'=12] {'fsdp'}, use_global_device_ids=true, to_apply=%region_4.7 | all-reduce | flops 256 | bytes 2048 | tf_op jit(solution)/shard_map/psum | solution.py:25
  434.3 129.1 %psum.66 = f32[8,8]{0,1:T(8,128)S(1)} all-reduce(f32[8,8]{0,1:T(8,128)S(1)} %fusion.34), channel_id=1, replica_groups=mesh['fsdp'=64,'dp'=12] {'fsdp'}, use_global_device_ids=true, to_apply=%region_5.8 | all-reduce | flops 64 | bytes 512 | tf_op jit(solution)/shard_map/psum | solution.py:32
  563.4 0.7 cholesky.85
  564.8 0.6 fusion.13
  566.4 241.2 %psum.67 = f32[32,8]{1,0:T(8,128)S(1)} all-reduce(f32[32,8]{1,0:T(8,128)S(1)} %fusion.26), channel_id=1, replica_groups=mesh['fsdp'=64,'dp'=12] {'fsdp'}, use_global_device_ids=true, to_apply=%region_6.9 | all-reduce | flops 256 | bytes 2048 | tf_op jit(solution)/shard_map/psum | solution.py:25
  807.9 129.1 %psum.68 = f32[8,8]{0,1:T(8,128)S(1)} all-reduce(f32[8,8]{0,1:T(8,128)S(1)} %fusion.35), channel_id=1, replica_groups=mesh['fsdp'=64,'dp'=12] {'fsdp'}, use_global_device_ids=true, to_apply=%region_7.10 | all-reduce | flops 64 | bytes 512 | tf_op jit(solution)/shard_map/psum | solution.py:32
  937.1 0.7 cholesky.96
  937.8 0.6 compare_reduce_fusion.1
  938.5 0.6 fusion.14
  940.1 241.2 %psum.69 = f32[32,8]{1,0:T(8,128)S(1)} all-reduce(f32[32,8]{1,0:T(8,128)S(1)} %fusion.24), channel_id=1, replica_groups=mesh['fsdp'=64,'dp'=12] {'fsdp'}, use_global_device_ids=true, to_apply=%region_8.11 | all-reduce | flops 256 | bytes 2048 | tf_op jit(solution)/shard_map/psum | solution.py:25
  1181.6 129.1 %psum.70 = f32[8,8]{0,1:T(8,128)S(1)} all-reduce(f32[8,8]{0,1:T(8,128)S(1)} %fusion.36), channel_id=1, replica_groups=mesh['fsdp'=64,'dp'=12] {'fsdp'}, use_global_device_ids=true, to_apply=%region_9.12 | all-reduce | flops 64 | bytes 512 | tf_op jit(solution)/shard_map/psum | solution.py:32
  1310.7 0.7 cholesky.107
  1311.5 0.6 compare_reduce_fusion
  1312.1 0.6 fusion.15
  1313.6 3.6 fusion.2
  1317.2 465.4 %all-reduce.3.cloned.1.call-done = f32[32,14336]{1,0:T(8,128)} async-done(((f32[32,14336]{1,0:T(8,128)}), f32[32,14336]{1,0:T(8,128)}) %all-reduce.3.cloned.1.call-update) | async-done | bytes 1835024 | tf_op jit(solution)/shard_map/psum | solution.py:48
  1782.6 1.8 broadcast_multiply_fusion
  1784.6 4.3 fusion.1
  (40 shorter events, 6.9 us)
Async XLA Ops:
  7.2 1.5 copy-start
  7.2 1775.4 %all-reduce.3.cloned.1.call-start = ((), (), s32[]{:S(2)}) async-start(), calls=%async_computation | async-start | bytes 3670016 | tf_op jit(solution)/shard_map/psum | solution.py:48
  1782.6 2.1 copy-start.1
  1784.6 4.3 copy-start.2
Sparse Core Ops, SparseCore 0:
  1317.3 465.1 all-reduce.2
where the time goes:
time: 1800 us
  blocking collectives  1290 us (72%)
  waiting for transfers between devices  465 us (26%)
    psum x3, blocking collectives, per_device(): lax.psum(jnp.dot(basis.T, columns, precision=HIGH, preferred_element_type...  723 us
    psum x4, blocking collectives, per_device(): lax.psum(jnp.dot(columns.T, columns, precision=HIGH, preferred_element_ty...  522 us
    psum x1, waiting for transfers between devices, per_device(): q_new = lax.psum(term, ('fsdp', 'dp')) / groups  465 us
    psum x1, blocking collectives, per_device(): left = lax.psum(local_left, 'dp')  42.8 us
  transfers between devices with their start and end apart: 1, of which 1 were waited for; matrix products, arithmetic and copies ran while one was open for 0% of the time, Pallas kernels for 0%

commit v1 on v0

v1 whole, which is shorter than its diff:
```python
import jax
import jax.numpy as jnp
from jax import lax
from jax.sharding import Mesh, PartitionSpec as P

HIGH = lax.Precision.HIGHEST
F32 = jnp.float32
NY, NX, NC = 8, 4, 2
TILE = 8
GRAM = 128


def spread(block, axis):
    count = lax.axis_size(axis)
    copies = jnp.broadcast_to(block[None], (count,) + block.shape)
    return lax.all_to_all(copies, axis, 0, 0, tiled=True)


def dot(a, b, contract):
    return lax.dot_general(a, b, ((contract[0:1], contract[1:2]), ((), ())), precision=HIGH, preferred_element_type=F32)


def per_device(grads, q_prev):
    corrected = grads[0].astype(F32)
    rank, cols = q_prev.shape
    rows = corrected.shape[0]
    groups = lax.axis_size("dp")
    wide = cols // (NC * NY)
    core = lax.axis_index("c")

    local = dot(q_prev, corrected, (1, 1))
    local = jnp.concatenate([local[: rank // 2], local[rank // 2 :]], axis=1)
    left_t = jnp.sum(spread(local, "dp"), axis=0)
    left_t = jnp.concatenate([left_t[:, :rows], left_t[:, rows:]], axis=0)

    gram = dot(left_t, left_t, (1, 1))
    gram = gram.reshape(NX, TILE, rank).transpose(1, 0, 2).reshape(TILE, GRAM)
    term = dot(left_t, corrected, (1, 0))
    term = term.reshape(NX, TILE, NC, NY, wide).transpose(2, 0, 3, 1, 4)
    tail = jnp.broadcast_to(gram, (NX, NY, TILE, GRAM))
    first = jnp.concatenate([term[0], tail], axis=-1)
    second = jnp.concatenate([term[1], tail], axis=-1)
    swap = [(0, 1), (1, 0)]
    other = lax.ppermute(jnp.where(core == 0, second, first), "c", swap)
    mine = jnp.where(core == 0, first, second) + other
    mine = mine.reshape(NX * NY, TILE, wide + GRAM)
    mine = jnp.sum(lax.all_to_all(mine, ("x", "y"), 0, 0, tiled=True), axis=0)
    gram = mine[:, wide:].reshape(TILE, NX, rank).transpose(1, 0, 2).reshape(rank, rank)
    block = jnp.sum(spread(mine[:, :wide], "dp"), axis=0)

    block = spread(block, "y")
    block = lax.all_gather(block, "x", axis=0)
    other = lax.ppermute(block, "c", swap)
    first = jnp.where(core == 0, block, other)
    second = jnp.where(core == 0, other, block)
    total = jnp.stack([first, second]).transpose(1, 3, 0, 2, 4).reshape(rank, cols)

    lower = jnp.linalg.cholesky(gram)
    inverse = lax.linalg.triangular_solve(lower, jnp.eye(rank, dtype=F32), left_side=True, lower=True)
    basis = dot(left_t, inverse, (0, 1))
    q_new = dot(inverse, total, (1, 0)) / groups
    resid_new = (corrected - dot(basis, q_new, (1, 0))).astype(jnp.bfloat16)
    return (q_new, resid_new[None])


def solution(mesh):
    groups = mesh.devices.shape[1]
    fine = Mesh(mesh.devices.reshape(NY, NX, NC, groups), ("y", "x", "c", "dp"))
    split = P("dp", ("y", "x", "c"), None)
    return jax.shard_map(per_device, mesh=fine, in_specs=(split, P()), out_specs=(P(), split), check_vma=False)
```

time: 1800 us -> 153 us (0.09)
  blocking collectives: 1290 us -> 61.7 us
  waiting for transfers between devices: 465 us -> 18.2 us
  starting transfers between devices: 0.04 us -> 38.9 us
    psum x8 -> x0, blocking collectives: 1290 us -> none  [the longest x3 723 us: per_device(): lax.psum(jnp.dot(basis.T, columns, precision=HIGH, preferred_element_type...]
    psum x1 -> x0, waiting for transfers between devices: 465 us -> none  [per_device(): q_new = lax.psum(term, ('fsdp', 'dp')) / groups]
    all_to_all x0 -> x2, blocking collectives: none -> 50.3 us  [the longest x1 34.7 us: per_device(): mine = jnp.sum(lax.all_to_all(mine, ('x', 'y'), 0, 0, tiled=True), axis=0)]
    all_to_all x0 -> x2, starting transfers between devices: none -> 25.1 us  [spread(): return lax.all_to_all(copies, axis, 0, 0, tiled=True)]
  transfers between devices with their start and end apart: 1 -> 4, of which waited for: 1 -> 3; matrix products, arithmetic and copies ran while one was open for 0% -> 7% of each run, Pallas kernels for 0% -> 0%
where the time goes in v1:
time: 153 us
  blocking collectives  61.7 us (40%)
  starting transfers between devices  38.9 us (25%)
  waiting for transfers between devices  18.2 us (12%)
  matrix products  13.6 us (9%)
  local copies, waits for them, and re-layouts  10.7 us (7%)
  other arithmetic  8.66 us (6%)
    all_to_all x1, blocking collectives, per_device(): mine = jnp.sum(lax.all_to_all(mine, ('x', 'y'), 0, 0, tiled=True), axis=0)  34.7 us
    all_to_all x2, starting transfers between devices, spread(): return lax.all_to_all(copies, axis, 0, 0, tiled=True)  25.1 us
    all_to_all x2, waiting for transfers between devices, spread(): return lax.all_to_all(copies, axis, 0, 0, tiled=True)  15.9 us
    all_to_all x1, blocking collectives, spread(): return lax.all_to_all(copies, axis, 0, 0, tiled=True)  15.7 us
    dot_general x6, matrix products, dot(): lax.dot_general(a, b, ((contract[0:1], contract[1:2]), ((), ())), precisi...  13.4 us
    all_gather x1, blocking collectives, per_device(): block = lax.all_gather(block, 'x', axis=0)  11.4 us
    ppermute x1, starting transfers between devices, per_device(): other = lax.ppermute(block, 'c', swap)  9.05 us
    ppermute x1, starting transfers between devices, per_device(): other = lax.ppermute(jnp.where(core == 0, second, first), 'c', swap)  4.8 us
  transfers between devices with their start and end apart: 4, of which 3 were waited for; matrix products, arithmetic and copies ran while one was open for 7% of the time, Pallas kernels for 0%

profile of v1, /device:TPU:1, one launch (start us, length us, event | category | flops | bytes accessed | tf_op | source)
XLA Modules:
  0.0 152.6 jit_solution(16644604709575147446)
XLA Ops:
  0.6 1.5 copy-done
  2.1 3.0 %fusion.4 = f32[32,64]{1,0:T(8,128)S(1)} fusion(f32[32,14336]{1,0:T(8,128)S(1)} %copy-done, bf16[1,64,14336]{2,1,0:T(8,128)(2,1)} %param.2), kind=kOutput, calls=%fused_computation.7 | convolution fusion | flops 352321536 | bytes 3678208 | tf_op jit(solution)/shard_map/dot_general | solution.py:20
  5.3 0.7 broadcast_in_dim.11
  5.9 15.7 %all-to-all-start = ((f32[12,16,128]{2,1,0:T(8,128)}), f32[12,16,128]{2,1,0:T(8,128)S(1)}, u32[]{:S(2)}, u32[]{:S(2)}) async-start(f32[12,16,128]{2,1,0:T(8,128)} %broadcast_in_dim.11), calls=%async_computation | async-start | bytes 196608 | tf_op jit(solution)/shard_map/all_to_all | solution.py:16
  21.6 3.0 %copy.34 = bf16[8,8,16,896]{3,2,1,0:T(8,128)(2,1)} copy(bf16[8,8,16,896]{3,1,2,0:T(8,128)(2,1)} %bitcast.68) | data formatting | bytes 3670016
  24.6 7.0 %all-to-all-done = f32[12,16,128]{2,1,0:T(8,128)S(1)} async-done(((f32[12,16,128]{2,1,0:T(8,128)}), f32[12,16,128]{2,1,0:T(8,128)S(1)}, u32[]{:S(2)}, u32[]{:S(2)}) %all-to-all-start) | async-done | bytes 98336 | tf_op jit(solution)/shard_map/all_to_all | solution.py:16
  32.0 2.5 %fusion.7 = f32[2,4,8,8,896]{4,3,2,0,1:T(8,128)S(1)} fusion(bf16[2,8,896,64]{2,1,0,3:T(8,128)(2,1)} %bitcast.69, f32[16,64]{1,0:T(8,128)S(1)} %get-tuple-element.9, f32[16,64]{1,0:T(8,128)S(1)} %get-tuple-element.8), kind=kOutput, calls=%fused_computation.10 | convolution fusion | flops 352323584 | bytes 3678208 | tf_op jit(solution)/shard_map/dot_general | solution.py:20
  34.8 4.8 %collective-permute-start = (f32[4,8,8,1024]{3,2,1,0:T(8,128)S(1)}, f32[4,8,8,1024]{3,2,1,0:T(8,128)S(1)}, u32[]{:S(2)}, u32[]{:S(2)}) collective-permute-start(f32[4,8,8,1024]{3,2,1,0:T(8,128)S(1)} %fusion.10), channel_id=1, source_target_pairs={{0,12},{12,0},{1,13},{13,1},{2,14},{14,2},{3,15},{15,3},{4,16},{16... | collective-permute-start | bytes 3145736 | tf_op jit(solution)/shard_map/ppermute | solution.py:44
  39.6 2.3 %collective-permute-done = f32[4,8,8,1024]{3,2,1,0:T(8,128)S(1)} collective-permute-done((f32[4,8,8,1024]{3,2,1,0:T(8,128)S(1)}, f32[4,8,8,1024]{3,2,1,0:T(8,128)S(1)}, u32[]{:S(2)}, u32[]{:S(2)}) %collective-permute-start) | collective-permute-done | bytes 1048608 | tf_op jit(solution)/shard_map/ppermute | solution.py:44
  42.1 34.7 %all_to_all.20 = f32[32,8,1024]{2,1,0:T(8,128)S(1)} all-to-all(f32[32,8,1024]{2,1,0:T(8,128)S(1)} %bitcast.70), channel_id=1, replica_groups=mesh['y'=8,'x'=4,'c'=2,'dp'=12] {'x','y'}, dimensions={0} | all-to-all | bytes 2097152 | tf_op jit(solution)/shard_map/all_to_all | solution.py:47
  76.9 15.7 %all_to_all.21 = f32[12,8,896]{2,1,0:T(8,128)S(1)} all-to-all(f32[12,8,896]{2,1,0:T(8,128)S(1)} %broadcast_in_dim.13), channel_id=1, replica_groups=mesh['y'=8,'x'=4,'c'=2,'dp'=12] {'dp'}, dimensions={0} | all-to-all | bytes 688128 | tf_op jit(solution)/shard_map/all_to_all | solution.py:16
  92.5 0.7 broadcast_in_dim.15
  93.2 9.3 %all-to-all-start.3 = ((f32[8,8,896]{2,1,0:T(8,128)}), f32[8,8,896]{2,1,0:T(8,128)S(1)}, u32[]{:S(2)}, u32[]{:S(2)}) async-start(f32[8,8,896]{2,1,0:T(8,128)} %broadcast_in_dim.15), calls=%async_computation.3 | async-start | bytes 458752 | tf_op jit(solution)/shard_map/all_to_all | solution.py:16
  102.8 8.8 %all-to-all-done.3 = f32[8,8,896]{2,1,0:T(8,128)S(1)} async-done(((f32[8,8,896]{2,1,0:T(8,128)}), f32[8,8,896]{2,1,0:T(8,128)S(1)}, u32[]{:S(2)}, u32[]{:S(2)}) %all-to-all-start.3) | async-done | bytes 229408 | tf_op jit(solution)/shard_map/all_to_all | solution.py:16
  111.6 11.4 %all-gather = f32[32,8,896]{2,1,0:T(8,128)S(1)} all-gather(f32[8,8,896]{2,1,0:T(8,128)S(1)} %all-to-all-done.3), channel_id=2, replica_groups=mesh['y'=8,'x'=4,'c'=2,'dp'=12] {'x'}, dimensions={0}, use_global_device_ids=true | all-gather | bytes 1146880 | tf_op jit(solution)/shard_map/all_gather | solution.py:52
  123.0 9.0 %collective-permute-start.1 = (f32[4,8,8,896]{3,2,1,0:T(8,128)S(1)}, f32[4,8,8,896]{3,2,1,0:T(8,128)}, u32[]{:S(2)}, u32[]{:S(2)}) collective-permute-start(f32[4,8,8,896]{3,2,1,0:T(8,128)S(1)} %bitcast.71), channel_id=1, source_target_pairs={{0,12},{12,0},{1,13},{13,1},{2,14},{14,2},{3,15},{15,3},{4,16},{16... | collective-permute-start | bytes 2752520 | tf_op jit(solution)/shard_map/ppermute | solution.py:53
  132.1 2.9 %cholesky.17 = f32[32,32]{1,0:T(8,128)S(1)} custom-call(f32[32,32]{1,0:T(8,128)S(1)} %fusion.15), custom_call_target="Cholesky" | custom-call | tf_op jit(solution)/shard_map/jit(cholesky)/cholesky | solution.py:58
  135.7 0.7 fusion.11
  136.3 2.4 %custom-call.6 = f32[1,32,32]{1,2,0:T(8,128)S(1)} custom-call(f32[1,32,32]{2,1,0:T(8,128)S(1)} %fusion.11), custom_call_target="InvertDiagBlocksLowerTriangular" | custom-call | tf_op jit(solution)/shard_map/triangular_solve | solution.py:59
  139.1 1.3 select_bitcast_fusion.1
  140.6 1.6 %copy.31 = f32[4,8,2,8,896]{4,3,2,1,0:T(8,128)} copy(f32[4,8,2,8,896]{4,1,3,0,2:T(8,128)S(1)} %maximum_bitcast_fusion) | data formatting | bytes 3670016 | tf_op jit(solution)/shard_map/transpose | solution.py:56
  142.2 2.8 %reshape.42 = f32[32,14336]{1,0:T(8,128)} reshape(f32[4,8,2,8,896]{4,3,2,1,0:T(8,128)} %copy.31) | data formatting | bytes 3670016 | tf_op jit(solution)/shard_map/reshape | solution.py:56
  145.0 3.3 %convolution_multiply_fusion = f32[32,14336]{1,0:T(8,128)S(1)} fusion(f32[32,32]{1,0:T(8,128)S(1)} %fusion.13, f32[32,14336]{1,0:T(8,128)} %reshape.42), kind=kOutput, calls=%fused_computation.3 | convolution fusion | flops 176619520 | bytes 3674112 | tf_op jit(solution)/shard_map/dot_general | solution.py:20
  148.3 4.3 %fusion.1 = bf16[1,64,14336]{2,1,0:T(8,128)(2,1)} fusion(f32[64,32]{0,1:T(8,128)S(1)} %fusion.16, f32[32,14336]{1,0:T(8,128)S(1)} %convolution_multiply_fusion, bf16[1,64,14336]{2,1,0:T(8,128)(2,1)S(1)} %copy-done.1), kind=kOutput, calls=%fused_computation.2 | convolution fusion | flops 355074048 | bytes 5513216 | tf_op jit(solution)/shard_map/dot_general | solution.py:20
  (31 shorter events, 2.4 us)
Async XLA Ops:
  0.6 1.5 copy-start
  5.9 25.7 %all-to-all-start = ((f32[12,16,128]{2,1,0:T(8,128)}), f32[12,16,128]{2,1,0:T(8,128)S(1)}, u32[]{:S(2)}, u32[]{:S(2)}) async-start(f32[12,16,128]{2,1,0:T(8,128)} %broadcast_in_dim.11), calls=%async_computation | async-start | bytes 196608 | tf_op jit(solution)/shard_map/all_to_all | solution.py:16
  34.8 7.1 %collective-permute-start = (f32[4,8,8,1024]{3,2,1,0:T(8,128)S(1)}, f32[4,8,8,1024]{3,2,1,0:T(8,128)S(1)}, u32[]{:S(2)}, u32[]{:S(2)}) collective-permute-start(f32[4,8,8,1024]{3,2,1,0:T(8,128)S(1)} %fusion.10), channel_id=1, source_target_pairs={{0,12},{12,0},{1,13},{13,1},{2,14},{14,2},{3,15},{15,3},{4,16},{16... | collective-permute-start | bytes 3145736 | tf_op jit(solution)/shard_map/ppermute | solution.py:44
  93.2 18.4 %all-to-all-start.3 = ((f32[8,8,896]{2,1,0:T(8,128)}), f32[8,8,896]{2,1,0:T(8,128)S(1)}, u32[]{:S(2)}, u32[]{:S(2)}) async-start(f32[8,8,896]{2,1,0:T(8,128)} %broadcast_in_dim.15), calls=%async_computation.3 | async-start | bytes 458752 | tf_op jit(solution)/shard_map/all_to_all | solution.py:16
  123.0 16.1 %collective-permute-start.1 = (f32[4,8,8,896]{3,2,1,0:T(8,128)S(1)}, f32[4,8,8,896]{3,2,1,0:T(8,128)}, u32[]{:S(2)}, u32[]{:S(2)}) collective-permute-start(f32[4,8,8,896]{3,2,1,0:T(8,128)S(1)} %bitcast.71), channel_id=1, source_target_pairs={{0,12},{12,0},{1,13},{13,1},{2,14},{14,2},{3,15},{15,3},{4,16},{16... | collective-permute-start | bytes 2752520 | tf_op jit(solution)/shard_map/ppermute | solution.py:53
  145.0 3.3 %copy-start.1 = (bf16[1,64,14336]{2,1,0:T(8,128)(2,1)S(1)}, bf16[1,64,14336]{2,1,0:T(8,128)(2,1)}, u32[]{:S(2)}) copy-start(bf16[1,64,14336]{2,1,0:T(8,128)(2,1)} %param.2) | copy-start | bytes 5505028
  148.3 4.3 %copy-start.2 = (f32[32,14336]{1,0:T(8,128)}, f32[32,14336]{1,0:T(8,128)S(1)}, u32[]{:S(2)}) copy-start(f32[32,14336]{1,0:T(8,128)S(1)} %convolution_multiply_fusion) | copy-start | bytes 5505028

commit v2 on v1

v2 whole, which is shorter than its diff:
```python
import functools

import jax
import jax.numpy as jnp
from jax import lax
from jax.experimental import pallas as pl
from jax.experimental.pallas import tpu as pltpu
from jax.sharding import Mesh, PartitionSpec as P

HIGH = lax.Precision.HIGHEST
F32, BF16 = jnp.float32, jnp.bfloat16
NY, NX, NC = 8, 4, 2
SUB, LANE = 8, 128
RANK = 32
TILES = 7
STEP = 14
WIDE = STEP * LANE
VMEM = 24 * 1024 * 1024


def params():
    return pltpu.CompilerParams(vmem_limit_bytes=VMEM, dimension_semantics=("arbitrary",))


def pieces(value, count):
    parts = []
    for _ in range(count):
        part = value.astype(BF16)
        parts.append(part)
        value = value - part.astype(F32)
    return parts


def dot(a, b, contract, precision=None):
    dims = ((contract[0:1], contract[1:2]), ((), ()))
    return lax.dot_general(a, b, dims, precision=precision, preferred_element_type=F32)


def left_of(shares_ref):
    packed = shares_ref[0]
    for g in range(1, shares_ref.shape[0]):
        packed = packed + shares_ref[g]
    half = LANE // 2
    return jnp.concatenate([packed[:, :half], packed[:, half:]], axis=0)


def project_kernel(grads_ref, q_ref, out_ref, acc_ref):
    step = pl.program_id(0)
    stack = jnp.concatenate(pieces(q_ref[...], 3), axis=0)
    part = dot(stack, grads_ref[0], (1, 1))

    @pl.when(step == 0)
    def _():
        acc_ref[...] = part

    @pl.when(step > 0)
    def _():
        acc_ref[...] += part

    @pl.when(step == pl.num_programs(0) - 1)
    def _():
        local = acc_ref[0:RANK] + acc_ref[RANK : 2 * RANK] + acc_ref[2 * RANK :]
        packed = jnp.concatenate([local[: RANK // 2], local[RANK // 2 :]], axis=1)
        for g in range(out_ref.shape[0]):
            out_ref[g] = packed


def project(grads, q_prev, groups):
    rows, cols = grads.shape[1:]
    wide = 2 * WIDE
    return pl.pallas_call(
        project_kernel,
        grid=(cols // wide,),
        in_specs=[
            pl.BlockSpec((1, rows, wide), lambda j: (0, 0, j)),
            pl.BlockSpec((RANK, wide), lambda j: (0, j)),
        ],
        out_specs=pl.BlockSpec((groups, RANK // 2, LANE), lambda j: (0, 0, 0)),
        out_shape=jax.ShapeDtypeStruct((groups, RANK // 2, LANE), F32),
        scratch_shapes=[pltpu.VMEM((3 * RANK, rows), F32)],
        compiler_params=params(),
        name="project",
    )(grads, q_prev)


def term_kernel(side_ref, shares_ref, grads_ref, out_ref):
    step = pl.program_id(0)
    left = left_of(shares_ref)
    stack = jnp.concatenate(pieces(left, 3), axis=0)
    part = dot(stack, grads_ref[0], (1, 0))
    part = part[:RANK] + part[RANK : 2 * RANK] + part[2 * RANK :]
    for x in range(NX):
        for t in range(STEP):
            out_ref[x, step * STEP + t] = part[x * SUB : (x + 1) * SUB, t * LANE : (t + 1) * LANE]

    @pl.when(step == 0)
    def _():
        wide = dot(left, jnp.concatenate([left] * NX, axis=0), (1, 1), HIGH)
        slot = lax.broadcasted_iota(jnp.int32, (SUB, LANE), 1) // RANK
        tile = jnp.zeros((SUB, LANE), F32)
        for x in range(NX):
            tile = jnp.where(slot == x, wide[x * SUB : (x + 1) * SUB], tile)
        for x in range(NX):
            out_ref[x, out_ref.shape[1] - 1] = tile


def term(side, shares, grads):
    rows, cols = grads.shape[1:]
    tiles = cols // NC // LANE
    steps = tiles // STEP
    shape = (NX, tiles + 1, SUB, LANE)
    return pl.pallas_call(
        term_kernel,
        grid_spec=pltpu.PrefetchScalarGridSpec(
            num_scalar_prefetch=1,
            grid=(steps,),
            in_specs=[
                pl.BlockSpec(shares.shape, lambda j, side: (0, 0, 0)),
                pl.BlockSpec((1, rows, WIDE), lambda j, side: (0, 0, side[0] * steps + j)),
            ],
            out_specs=pl.BlockSpec(shape, lambda j, side: (0, 0, 0, 0)),
        ),
        out_shape=jax.ShapeDtypeStruct(shape, F32),
        compiler_params=params(),
        cost_estimate=pl.CostEstimate(flops=2 * 96 * rows * cols // NC, bytes_accessed=3 * rows * cols, transcendentals=0),
        name="term",
    )(side, shares, grads)


def factor_kernel(gram_ref, shares_ref, inverse_ref, basis_ref):
    tile = gram_ref[...]
    lane = lax.broadcasted_iota(jnp.int32, (RANK, LANE), 1)
    row = lax.broadcasted_iota(jnp.int32, (RANK, LANE), 0)
    work = jnp.concatenate([pltpu.roll(tile, (LANE - RANK * x) % LANE, 1) for x in range(NX)], axis=0)
    work = jnp.where(lane < RANK, work, jnp.where(lane - RANK == row, 1.0, 0.0))
    for k in range(RANK):
        scale = 1.0 / jnp.sqrt(work[k : k + 1, k : k + 1])
        across = work[k : k + 1] * scale
        down = work[:, k : k + 1] * scale
        work = jnp.where(row > k, work - down * across, jnp.where(row == k, across, work))
    inverse = jnp.where(lane < RANK, pltpu.roll(work, LANE - RANK, 1), 0.0)
    one, two, three = [part.astype(F32) for part in pieces(inverse, 3)]

    def at(value, slot):
        return pltpu.roll(value, RANK * slot, 1) if slot else value

    inverse_ref[:, :LANE] = (at(one, 0) + at(one, 1) + at(two, 2) + at(one, 3)).astype(BF16)
    inverse_ref[:, LANE:] = (at(two, 0) + at(three, 1)).astype(BF16)
    basis = dot(left_of(shares_ref), jnp.concatenate([inverse[:, :RANK]] * 4, axis=0), (0, 1), HIGH)
    high = basis.astype(BF16).astype(F32)
    wide = lax.broadcasted_iota(jnp.int32, basis.shape, 1)
    basis_ref[...] = jnp.where(wide < LANE // 2, high, basis - high).astype(BF16)


def factor(gram, shares, rows):
    return pl.pallas_call(
        factor_kernel,
        out_shape=(
            jax.ShapeDtypeStruct((RANK, 2 * LANE), BF16),
            jax.ShapeDtypeStruct((rows, LANE), BF16),
        ),
        compiler_params=pltpu.CompilerParams(vmem_limit_bytes=VMEM),
        cost_estimate=pl.CostEstimate(flops=1 << 22, bytes_accessed=1 << 20, transcendentals=32),
        name="factor",
    )(gram, shares)


def finish_kernel(groups, side_ref, total_ref, inverse_ref, basis_ref, grads_ref, *rest):
    q_ref, resid_ref = rest[-2:]
    total = jnp.concatenate(
        [jnp.concatenate([total_ref[x, t] for x in range(NX)], axis=0) for t in range(STEP)], axis=1
    )
    one, two, three = pieces(total, 3)
    stack = jnp.concatenate([one, two, one, three, two, one, one, one], axis=0)
    q_new = dot(inverse_ref[...], stack, (1, 0)) / groups
    q_ref[...] = q_new
    high, low = pieces(q_new, 2)
    approx = dot(basis_ref[...], jnp.concatenate([high, low, high, low], axis=0), (1, 0))
    resid_ref[0] = (grads_ref[0].astype(F32) - approx).astype(BF16)


def finish(side, total, inverse, basis, grads, groups, partial=()):
    rows, cols = grads.shape[1:]
    steps = total.shape[1] // STEP
    whole = lambda j, side: (0, 0)
    return pl.pallas_call(
        functools.partial(finish_kernel, groups),
        grid_spec=pltpu.PrefetchScalarGridSpec(
            num_scalar_prefetch=1,
            grid=(steps,),
            in_specs=[
                pl.BlockSpec((NX, STEP, SUB, LANE), lambda j, side: (0, j, 0, 0)),
                pl.BlockSpec(inverse.shape, whole),
                pl.BlockSpec(basis.shape, whole),
                pl.BlockSpec((1, rows, WIDE), lambda j, side: (0, 0, side[0] * steps + j)),
            ]
            + [pl.BlockSpec(memory_space=pl.ANY)] * len(partial),
            out_specs=[
                pl.BlockSpec((RANK, WIDE), lambda j, side: (0, side[0] * steps + j)),
                pl.BlockSpec((1, rows, WIDE), lambda j, side: (0, 0, side[0] * steps + j)),
            ],
        ),
        out_shape=(
            jax.ShapeDtypeStruct((RANK, cols), F32),
            jax.ShapeDtypeStruct((1, rows, cols), BF16),
        ),
        input_output_aliases={5: 0, 6: 1} if partial else {},
        compiler_params=params(),
        cost_estimate=pl.CostEstimate(flops=2 * 160 * rows * cols // NC, bytes_accessed=6 * rows * cols, transcendentals=0),
        name="finish",
    )(side, total, inverse, basis, grads, *partial)


def exchange(blocks, axis):
    return lax.all_to_all(blocks, axis, 0, 0, tiled=True)


def spread(block, axis):
    return exchange(jnp.broadcast_to(block[None], (lax.axis_size(axis),) + block.shape), axis)


def per_device(grads, q_prev):
    groups = lax.axis_size("dp")
    core = lax.axis_index("c").astype(jnp.int32)
    own = core.reshape(1)
    other = 1 - own
    swap = [(0, 1), (1, 0)]

    shares = exchange(project(grads, q_prev, groups), "dp")
    away = lax.ppermute(term(other, shares, grads), "c", swap)
    part = term(own, shares, grads) + away
    part = jnp.sum(exchange(part, "x"), axis=0)
    tail = jnp.broadcast_to(part[-1], (NY, 1, SUB, LANE))
    part = jnp.concatenate([part[:-1].reshape(NY, TILES, SUB, LANE), tail], axis=1)
    part = jnp.sum(exchange(part, "y"), axis=0)
    inverse, basis = factor(part[TILES], shares, grads.shape[1])
    part = jnp.sum(spread(part[:TILES], "dp"), axis=0)

    total = spread(part, "y").reshape(NY * TILES, SUB, LANE)
    total = lax.all_gather(total, "x", axis=0)
    away = lax.ppermute(total, "c", swap)
    mine = finish(own, total, inverse, basis, grads, groups)
    return tuple(finish(other, away, inverse, basis, grads, groups, mine))


def solution(mesh):
    groups = mesh.devices.shape[1]
    fine = Mesh(mesh.devices.reshape(NY, NX, NC, groups), ("y", "x", "c", "dp"))
    split = P("dp", ("y", "x", "c"), None)
    return jax.shard_map(per_device, mesh=fine, in_specs=(split, P()), out_specs=(P(), split), check_vma=False)
```

time: 153 us -> 135 us (0.88)
  Pallas kernels: 0 us -> 14.5 us
  matrix products: 13.6 us -> 0 us
  blocking collectives: 61.7 us -> 74.4 us
  other arithmetic: 8.66 us -> 0.24 us
  starting transfers between devices: 38.9 us -> 30.5 us
  local copies, waits for them, and re-layouts: 10.7 us -> 3.07 us
  waiting for transfers between devices: 18.2 us -> 10.6 us
    pallas_call x0 -> x6, Pallas kernels: none -> 14.5 us  [the longest x2 5.74 us: finish(): pl.pallas_call(functools.partial(finish_kernel, groups), grid_spec=pltpu....]
    dot_general x6 -> x0, matrix products: 13.4 us -> none  [dot(): lax.dot_general(a, b, ((contract[0:1], contract[1:2]), ((), ())), precisi...]
    all_to_all x2 -> x4, blocking collectives: 50.3 us -> 62.7 us  [exchange(): return lax.all_to_all(blocks, axis, 0, 0, tiled=True)]
    all_to_all x2 -> x1, starting transfers between devices: 25.1 us -> 15.7 us  [exchange(): return lax.all_to_all(blocks, axis, 0, 0, tiled=True)]
    another operation x6 -> x0, other arithmetic: 8 us -> none  [the longest x3 3.59 us: per_device(): lower = jnp.linalg.cholesky(gram)]
    all_to_all x2 -> x1, waiting for transfers between devices: 15.9 us -> 10 us  [exchange(): return lax.all_to_all(blocks, axis, 0, 0, tiled=True)]
    reshape x4 -> x0, local copies, waits for them, and re-layouts: 3.01 us -> none  [the longest x1 2.77 us: per_device(): jnp.stack([first, second]).transpose(1, 3, 0, 2, 4).reshape(rank, cols)]
    ppermute x2, waiting for transfers between devices: 2.28 us -> 0.58 us  [the longest x1 0.58 us: per_device(): away = lax.ppermute(term(other, shares, grads), 'c', swap)]
  transfers between devices with their start and end apart: 4 -> 3, of which waited for: 3 -> 2; matrix products, arithmetic and copies ran while one was open for 7% -> 0% of each run, Pallas kernels for 0% -> 6%
where the time goes in v2:
time: 135 us; the launch traced here: 134 us
  blocking collectives  74.4 us (55%)
  starting transfers between devices  30.5 us (23%)
  Pallas kernels  14.5 us (11%)
  waiting for transfers between devices  10.6 us (8%)
  local copies, waits for them, and re-layouts  3.07 us (2%)
    all_to_all x4, blocking collectives, exchange(): return lax.all_to_all(blocks, axis, 0, 0, tiled=True)  62.7 us
    all_to_all x1, starting transfers between devices, exchange(): return lax.all_to_all(blocks, axis, 0, 0, tiled=True)  15.7 us
    all_gather x1, blocking collectives, per_device(): total = lax.all_gather(total, 'x', axis=0)  11.7 us
    all_to_all x1, waiting for transfers between devices, exchange(): return lax.all_to_all(blocks, axis, 0, 0, tiled=True)  10 us
    ppermute x1, starting transfers between devices, per_device(): away = lax.ppermute(total, 'c', swap)  10 us
    pallas_call x2, Pallas kernels, finish(): pl.pallas_call(functools.partial(finish_kernel, groups), grid_spec=pltpu....  5.74 us
    ppermute x1, starting transfers between devices, per_device(): away = lax.ppermute(term(other, shares, grads), 'c', swap)  4.79 us
    pallas_call x1, Pallas kernels, factor(): pl.pallas_call(factor_kernel, out_shape=(jax.ShapeDtypeStruct((RANK, 2 *...  3.34 us
  transfers between devices with their start and end apart: 3, of which 2 were waited for; matrix products, arithmetic and copies ran while one was open for 0% of the time, Pallas kernels for 6%

profile of v2, /device:TPU:1, one launch (start us, length us, event | category | flops | bytes accessed | tf_op | source)
XLA Modules:
  0.0 134.1 jit_solution(2038685720104638844)
XLA Ops:
  0.6 0.0 copy-start
  0.6 1.5 %copy-done = bf16[1,64,14336]{2,1,0:T(8,128)(2,1)S(1)} copy-done((bf16[1,64,14336]{2,1,0:T(8,128)(2,1)S(1)}, bf16[1,64,14336]{2,1,0:T(8,128)(2,1)}, u32[]{:S(2)}) %copy-start) | copy-done | bytes 1835032
  2.1 0.0 copy-start.2
  2.1 1.5 %copy-done.2 = f32[32,14336]{1,0:T(8,128)S(1)} copy-done((f32[32,14336]{1,0:T(8,128)S(1)}, f32[32,14336]{1,0:T(8,128)}, u32[]{:S(2)}) %copy-start.2) | copy-done | bytes 1835032
  3.6 2.4 %project.1 = f32[12,16,128]{2,1,0:T(8,128)} custom-call(bf16[1,64,14336]{2,1,0:T(8,128)(2,1)S(1)} %copy-done, f32[32,14336]{1,0:T(8,128)S(1)} %copy-done.2), custom_call_target="tpu_custom_call" | custom-call | tf_op jit(solution)/shard_map/project/pallas_call | solution.py:71
  6.1 15.7 %all-to-all-start = ((f32[12,16,128]{2,1,0:T(8,128)}), f32[12,16,128]{2,1,0:T(8,128)S(1)}, u32[]{:S(2)}, u32[]{:S(2)}) async-start(f32[12,16,128]{2,1,0:T(8,128)} %project.1), calls=%async_computation | async-start | bytes 196608 | tf_op jit(solution)/shard_map/all_to_all | solution.py:215
  21.8 10.0 %all-to-all-done.shares_ref = f32[12,16,128]{2,1,0:T(8,128)S(1)} async-done(((f32[12,16,128]{2,1,0:T(8,128)}), f32[12,16,128]{2,1,0:T(8,128)S(1)}, u32[]{:S(2)}, u32[]{:S(2)}) %all-to-all-start) | async-done | bytes 98336 | tf_op jit(solution)/shard_map/all_to_all | solution.py:215
  31.8 0.0 copy-done.1
  31.8 1.5 %term.3 = f32[4,57,8,128]{3,2,1,0:T(8,128)S(1)} custom-call(s32[1]{0:T(128)S(6)} %sub.3.side_ref, f32[12,16,128]{2,1,0:T(8,128)S(1)} %all-to-all-done.shares_ref, bf16[1,64,14336]{2,1,0:T(8,128)(2,1)S(1)} %copy-done.1), custom_call_target="tpu_custom_call" | custom-call | flops 88080384 | bytes 2752512 | tf_op jit(solution)/shard_map/term/pallas_call | solution.py:112
  33.3 4.8 %collective-permute-start = (f32[4,57,8,128]{3,2,1,0:T(8,128)S(1)}, f32[4,57,8,128]{3,2,1,0:T(8,128)S(1)}, u32[]{:S(2)}, u32[]{:S(2)}) collective-permute-start(f32[4,57,8,128]{3,2,1,0:T(8,128)S(1)} %term.3), channel_id=1, source_target_pairs={{0,12},{12,0},{1,13},{13,1},{2,14},{14,2},{3,15},{15,3},{4,16},{16... | collective-permute-start | bytes 2801672 | tf_op jit(solution)/shard_map/ppermute | solution.py:230
  38.1 1.5 %term.2 = f32[4,57,8,128]{3,2,1,0:T(8,128)S(1)} custom-call(s32[1]{0:T(128)} %bitcast.side_ref, f32[12,16,128]{2,1,0:T(8,128)S(1)} %all-to-all-done.shares_ref, bf16[1,64,14336]{2,1,0:T(8,128)(2,1)S(1)} %copy-done.1), custom_call_target="tpu_custom_call" | custom-call | flops 88080384 | bytes 2752512 | tf_op jit(solution)/shard_map/term/pallas_call | solution.py:112
  39.6 0.6 collective-permute-done
  40.2 0.1 add.3
  40.3 17.1 %all_to_all.25 = f32[4,57,8,128]{3,2,1,0:T(8,128)S(1)} all-to-all(f32[4,57,8,128]{3,2,1,0:T(8,128)S(1)} %add.3), channel_id=1, replica_groups=mesh['y'=8,'x'=4,'c'=2,'dp'=12] {'x'}, dimensions={0} | all-to-all | bytes 1867776 | tf_op jit(solution)/shard_map/all_to_all | solution.py:215
  57.4 0.1 reduce_sum.27
  57.6 16.1 %all_to_all.26 = f32[8,8,8,128]{3,2,1,0:T(8,128)S(1)} all-to-all(f32[8,8,8,128]{3,2,1,0:T(8,128)S(1)} %pad_maximum_fusion), channel_id=1, replica_groups=mesh['y'=8,'x'=4,'c'=2,'dp'=12] {'y'}, dimensions={0} | all-to-all | bytes 524288 | tf_op jit(solution)/shard_map/all_to_all | solution.py:215
  73.7 16.3 %all_to_all.27 = f32[12,7,8,128]{3,2,1,0:T(8,128)S(1)} all-to-all(f32[12,7,8,128]{3,2,1,0:T(8,128)S(1)} %broadcast_in_dim.7), channel_id=1, replica_groups=mesh['y'=8,'x'=4,'c'=2,'dp'=12] {'dp'}, dimensions={0} | all-to-all | bytes 688128 | tf_op jit(solution)/shard_map/all_to_all | solution.py:215
  90.1 13.2 %all_to_all.28 = f32[8,7,8,128]{3,2,1,0:T(8,128)S(1)} all-to-all(f32[8,7,8,128]{3,2,1,0:T(8,128)S(1)} %broadcast_in_dim.8), channel_id=1, replica_groups=mesh['y'=8,'x'=4,'c'=2,'dp'=12] {'y'}, dimensions={0} | all-to-all | bytes 458752 | tf_op jit(solution)/shard_map/all_to_all | solution.py:215
  103.3 11.7 %all_gather.3.total_ref = f32[4,56,8,128]{3,2,1,0:T(8,128)S(1)} all-gather(f32[1,56,8,128]{3,2,1,0:T(8,128)S(1)} %bitcast.8), channel_id=1, replica_groups=mesh['y'=8,'x'=4,'c'=2,'dp'=12] {'x'}, dimensions={0}, use_global_device_ids=true | all-gather | bytes 1146880 | tf_op jit(solution)/shard_map/all_gather | solution.py:240
  115.0 10.0 %collective-permute-start.1 = (f32[4,56,8,128]{3,2,1,0:T(8,128)S(1)}, f32[4,56,8,128]{3,2,1,0:T(8,128)S(1)}, u32[]{:S(2)}, u32[]{:S(2)}) collective-permute-start(f32[4,56,8,128]{3,2,1,0:T(8,128)S(1)} %all_gather.3.total_ref), channel_id=1, source_target_pairs={{0,12},{12,0},{1,13},{13,1},{2,14},{14,2},{3,15},{15,3},{4,16},{16... | collective-permute-start | bytes 2752520 | tf_op jit(solution)/shard_map/ppermute | solution.py:241
  125.0 3.3 %factor.1 = (bf16[32,256]{1,0:T(8,128)(2,1)S(1)}, bf16[64,128]{1,0:T(8,128)(2,1)S(1)}) custom-call(f32[8,128]{1,0:T(8,128)S(1)} %slice_bitcast_fusion.gram_ref, f32[12,16,128]{2,1,0:T(8,128)S(1)} %all-to-all-done.shares_ref), custom_call_target="tpu_custom_call" | custom-call | flops 4194304 | bytes 1048576 | tf_op jit(solution)/shard_map/factor/pallas_call | solution.py:156
  128.4 2.9 %finish.2 = (f32[32,14336]{1,0:T(8,128)}, bf16[1,64,14336]{2,1,0:T(8,128)(2,1)}) custom-call(s32[1]{0:T(128)} %bitcast.side_ref, f32[4,56,8,128]{3,2,1,0:T(8,128)S(1)} %all_gather.3.total_ref, bf16[32,256]{1,0:T(8,128)(2,1)S(1)} %get-tuple-element.6.inverse_ref, bf16[64,128]{1,0:T(8,128)(2,1)S(1)} %get-tuple-element.7.basis_ref, ...), custom_call_target="tpu_custom_call" | custom-call | flops 146800640 | bytes 5505024 | tf_op jit(solution)/shard_map/finish/pallas_call | solution.py:186
  131.2 0.0 collective-permute-done.1.total_ref
  131.2 2.9 %finish.3 = (f32[32,14336]{1,0:T(8,128)}, bf16[1,64,14336]{2,1,0:T(8,128)(2,1)}) custom-call(s32[1]{0:T(128)S(6)} %sub.3.side_ref, f32[4,56,8,128]{3,2,1,0:T(8,128)S(1)} %collective-permute-done.1.total_ref, bf16[32,256]{1,0:T(8,128)(2,1)S(1)} %get-tuple-element.6.inverse_ref, ...), custom_call_target="tpu_custom_call", output_to_operand_aliasing={{0}: (5, {}), {1}: (6, {})} | custom-call | flops 146800640 | bytes 5505024 | tf_op jit(solution)/shard_map/finish/pallas_call | solution.py:186
  (11 shorter events, 0.1 us)
Async XLA Ops:
  0.6 1.5 %copy-start = (bf16[1,64,14336]{2,1,0:T(8,128)(2,1)S(1)}, bf16[1,64,14336]{2,1,0:T(8,128)(2,1)}, u32[]{:S(2)}) copy-start(bf16[1,64,14336]{2,1,0:T(8,128)(2,1)} %grads_ref.9) | copy-start | bytes 5505028
  2.1 1.5 %copy-start.2 = (f32[32,14336]{1,0:T(8,128)S(1)}, f32[32,14336]{1,0:T(8,128)}, u32[]{:S(2)}) copy-start(f32[32,14336]{1,0:T(8,128)} %q_ref.1) | copy-start | bytes 5505028
  3.6 28.2 %copy-start.1 = (bf16[1,64,14336]{2,1,0:T(8,128)(2,1)S(1)}, bf16[1,64,14336]{2,1,0:T(8,128)(2,1)}, u32[]{:S(2)}) copy-start(bf16[1,64,14336]{2,1,0:T(8,128)(2,1)} %grads_ref.9) | copy-start | bytes 5505028
  6.1 25.8 %all-to-all-start = ((f32[12,16,128]{2,1,0:T(8,128)}), f32[12,16,128]{2,1,0:T(8,128)S(1)}, u32[]{:S(2)}, u32[]{:S(2)}) async-start(f32[12,16,128]{2,1,0:T(8,128)} %project.1), calls=%async_computation | async-start | bytes 196608 | tf_op jit(solution)/shard_map/all_to_all | solution.py:215
  33.3 6.9 %collective-permute-start = (f32[4,57,8,128]{3,2,1,0:T(8,128)S(1)}, f32[4,57,8,128]{3,2,1,0:T(8,128)S(1)}, u32[]{:S(2)}, u32[]{:S(2)}) collective-permute-start(f32[4,57,8,128]{3,2,1,0:T(8,128)S(1)} %term.3), channel_id=1, source_target_pairs={{0,12},{12,0},{1,13},{13,1},{2,14},{14,2},{3,15},{15,3},{4,16},{16... | collective-permute-start | bytes 2801672 | tf_op jit(solution)/shard_map/ppermute | solution.py:230
  115.0 16.3 %collective-permute-start.1 = (f32[4,56,8,128]{3,2,1,0:T(8,128)S(1)}, f32[4,56,8,128]{3,2,1,0:T(8,128)S(1)}, u32[]{:S(2)}, u32[]{:S(2)}) collective-permute-start(f32[4,56,8,128]{3,2,1,0:T(8,128)S(1)} %all_gather.3.total_ref), channel_id=1, source_target_pairs={{0,12},{12,0},{1,13},{13,1},{2,14},{14,2},{3,15},{15,3},{4,16},{16... | collective-permute-start | bytes 2752520 | tf_op jit(solution)/shard_map/ppermute | solution.py:241

commit v3 on v2

v3 whole, which is shorter than its diff:
```python
import functools

import jax
import jax.numpy as jnp
from jax import lax
from jax.experimental import pallas as pl
from jax.experimental.pallas import tpu as pltpu
from jax.sharding import Mesh, PartitionSpec as P

HIGH = lax.Precision.HIGHEST
F32, BF16 = jnp.float32, jnp.bfloat16
NY, NX, NC = 8, 4, 2
SUB, LANE = 8, 128
RANK = 32
TILES = 7
STEP = 28
WIDE = STEP * LANE
COPIES = 2
AHEAD = 4
VMEM = 24 * 1024 * 1024


def params():
    return pltpu.CompilerParams(vmem_limit_bytes=VMEM, dimension_semantics=("arbitrary",))


def pieces(value, count):
    parts = []
    for _ in range(count):
        part = value.astype(BF16)
        parts.append(part)
        value = value - part.astype(F32)
    return parts


def dot(a, b, contract, precision=None):
    dims = ((contract[0:1], contract[1:2]), ((), ()))
    return lax.dot_general(a, b, dims, precision=precision, preferred_element_type=F32)


def left_of(shares_ref):
    packed = shares_ref[0]
    for g in range(1, shares_ref.shape[0]):
        packed = packed + shares_ref[g]
    half = LANE // 2
    return jnp.concatenate([packed[:, :half], packed[:, half:]], axis=0)


def project_kernel(own_ref, grads_ref, q_ref, out_ref, grads_buf, sides_ref, q_buf, sems):
    sides_ref[0] = own_ref[0]
    sides_ref[1] = 1 - own_ref[0]
    count = sems.shape[0]
    wide = q_buf.shape[1] // count
    copies = []
    for n in range(count):
        cols = pl.ds(n * wide, wide)
        copies.append(
            (
                pltpu.make_async_copy(grads_ref.at[:, :, cols], grads_buf.at[:, :, cols], sems.at[n, 0]),
                pltpu.make_async_copy(q_ref.at[:, cols], q_buf.at[:, cols], sems.at[n, 1]),
            )
        )
        for copy in copies[-1]:
            copy.start()
    total = None
    for n in range(count):
        for copy in copies[n]:
            copy.wait()
        cols = pl.ds(n * wide, wide)
        stack = jnp.concatenate(pieces(q_buf[:, cols], 3), axis=0)
        part = dot(stack, grads_buf[0, :, cols], (1, 1))
        total = part if total is None else total + part
    local = total[:RANK] + total[RANK : 2 * RANK] + total[2 * RANK :]
    packed = jnp.concatenate([local[: RANK // 2], local[RANK // 2 :]], axis=1)
    for g in range(out_ref.shape[0]):
        out_ref[g] = packed


def project(own, grads, q_prev, groups):
    rows, cols = grads.shape[1:]
    return pl.pallas_call(
        project_kernel,
        in_specs=[pl.BlockSpec(memory_space=pltpu.SMEM)] + [pl.BlockSpec(memory_space=pl.ANY)] * 2,
        out_specs=(
            pl.BlockSpec(memory_space=pltpu.VMEM),
            pl.BlockSpec(memory_space=pltpu.VMEM),
            pl.BlockSpec(memory_space=pltpu.SMEM),
        ),
        out_shape=(
            jax.ShapeDtypeStruct((groups, RANK // 2, LANE), F32),
            pltpu.VMEM(grads.shape, BF16),
            jax.ShapeDtypeStruct((2,), jnp.int32),
        ),
        scratch_shapes=[
            pltpu.VMEM((RANK, cols), F32),
            pltpu.SemaphoreType.DMA((COPIES, 2)),
        ],
        compiler_params=pltpu.CompilerParams(vmem_limit_bytes=VMEM),
        name="project",
    )(own, pltpu.with_memory_space_constraint(grads, pltpu.HBM), pltpu.with_memory_space_constraint(q_prev, pltpu.HBM))


def term_kernel(sides_ref, shares_ref, grads_ref, out_ref):
    left = left_of(shares_ref)
    stack = jnp.concatenate(pieces(left, 3), axis=0)
    part = dot(stack, grads_ref[0], (1, 0))
    part = part[:RANK] + part[RANK : 2 * RANK] + part[2 * RANK :]
    tiles = out_ref.shape[1] - 1
    wide = dot(left, jnp.concatenate([left] * NX, axis=0), (1, 1), HIGH)
    slot = lax.broadcasted_iota(jnp.int32, (SUB, LANE), 1) // RANK
    tile = jnp.zeros((SUB, LANE), F32)
    for x in range(NX):
        tile = jnp.where(slot == x, wide[x * SUB : (x + 1) * SUB], tile)
    for x in range(NX):
        for t in range(tiles):
            out_ref[x, t] = part[x * SUB : (x + 1) * SUB, t * LANE : (t + 1) * LANE]
        out_ref[x, tiles] = tile


def term(side, sides, shares, grads):
    rows, cols = grads.shape[1:]
    half = cols // NC
    shape = (NX, half // LANE + 1, SUB, LANE)
    return pl.pallas_call(
        term_kernel,
        grid_spec=pltpu.PrefetchScalarGridSpec(
            num_scalar_prefetch=1,
            grid=(1,),
            in_specs=[
                pl.BlockSpec(shares.shape, lambda j, sides: (0, 0, 0)),
                pl.BlockSpec((1, rows, half), lambda j, sides: (0, 0, sides[side])),
            ],
            out_specs=pl.BlockSpec(shape, lambda j, sides: (0, 0, 0, 0)),
        ),
        out_shape=jax.ShapeDtypeStruct(shape, F32),
        compiler_params=params(),
        cost_estimate=pl.CostEstimate(flops=2 * 96 * rows * half, bytes_accessed=6 * rows * half, transcendentals=0),
        name="term",
    )(sides, shares, grads)


def factor_kernel(gram_ref, shares_ref, inverse_ref, basis_ref):
    tile = gram_ref[...]
    lane = lax.broadcasted_iota(jnp.int32, (RANK, LANE), 1)
    row = lax.broadcasted_iota(jnp.int32, (RANK, LANE), 0)
    work = jnp.concatenate([pltpu.roll(tile, (LANE - RANK * x) % LANE, 1) for x in range(NX)], axis=0)
    work = jnp.where(lane < RANK, work, jnp.where(lane - RANK == row, 1.0, 0.0))
    for k in range(0, RANK, AHEAD):
        downs = [jnp.broadcast_to(work[:, j : j + 1], work.shape) for j in range(k, k + AHEAD)]
        rights = [work[j : j + 1] for j in range(k, k + AHEAD)]
        for j in range(AHEAD):
            down = downs[j]
            scale = 1.0 / down[k + j : k + j + 1]
            across = rights[j] * scale
            for i in range(j + 1, AHEAD):
                ratio = down[k + i : k + i + 1]
                rights[i] = rights[i] - ratio * across
                downs[i] = downs[i] - down * (ratio * scale)
            work = jnp.where(row > k + j, work - down * across, work)
    pivots = jnp.sum(jnp.where(lane == row, work, 0.0), axis=1, keepdims=True)
    work = work * (1.0 / jnp.sqrt(pivots))
    inverse = jnp.where(lane < RANK, pltpu.roll(work, LANE - RANK, 1), 0.0)
    one, two, three = [part.astype(F32) for part in pieces(inverse, 3)]

    def at(value, slot):
        return pltpu.roll(value, RANK * slot, 1) if slot else value

    inverse_ref[:, :LANE] = (at(one, 0) + at(one, 1) + at(two, 2) + at(one, 3)).astype(BF16)
    inverse_ref[:, LANE:] = (at(two, 0) + at(three, 1)).astype(BF16)
    basis = dot(left_of(shares_ref), jnp.concatenate([inverse[:, :RANK]] * 4, axis=0), (0, 1), HIGH)
    high = basis.astype(BF16).astype(F32)
    wide = lax.broadcasted_iota(jnp.int32, basis.shape, 1)
    basis_ref[...] = jnp.where(wide < LANE // 2, high, basis - high).astype(BF16)


def factor(gram, shares, rows):
    return pl.pallas_call(
        factor_kernel,
        out_shape=(
            jax.ShapeDtypeStruct((RANK, 2 * LANE), BF16),
            jax.ShapeDtypeStruct((rows, LANE), BF16),
        ),
        compiler_params=pltpu.CompilerParams(vmem_limit_bytes=VMEM),
        cost_estimate=pl.CostEstimate(flops=1 << 22, bytes_accessed=1 << 20, transcendentals=32),
        name="factor",
    )(gram, shares)


def finish_kernel(groups, sides_ref, total_ref, inverse_ref, basis_ref, grads_ref, *rest):
    q_ref, resid_ref = rest[-2:]
    total = jnp.concatenate(
        [jnp.concatenate([total_ref[x, t] for x in range(NX)], axis=0) for t in range(STEP)], axis=1
    )
    one, two, three = pieces(total, 3)
    stack = jnp.concatenate([one, two, one, three, two, one, one, one], axis=0)
    q_new = dot(inverse_ref[...], stack, (1, 0)) / groups
    q_ref[...] = q_new
    high, low = pieces(q_new, 2)
    approx = dot(basis_ref[...], jnp.concatenate([high, low, high, low], axis=0), (1, 0))
    resid_ref[0] = (grads_ref[0].astype(F32) - approx).astype(BF16)


def finish(side, sides, total, inverse, basis, grads, groups, partial=()):
    rows, cols = grads.shape[1:]
    steps = total.shape[1] // STEP
    whole = lambda j, sides: (0, 0)
    return pl.pallas_call(
        functools.partial(finish_kernel, groups),
        grid_spec=pltpu.PrefetchScalarGridSpec(
            num_scalar_prefetch=1,
            grid=(steps,),
            in_specs=[
                pl.BlockSpec((NX, STEP, SUB, LANE), lambda j, sides: (0, j, 0, 0)),
                pl.BlockSpec(inverse.shape, whole),
                pl.BlockSpec(basis.shape, whole),
                pl.BlockSpec((1, rows, WIDE), lambda j, sides: (0, 0, sides[side] * steps + j)),
            ]
            + [pl.BlockSpec(memory_space=pl.ANY)] * len(partial),
            out_specs=[
                pl.BlockSpec((RANK, WIDE), lambda j, sides: (0, sides[side] * steps + j)),
                pl.BlockSpec((1, rows, WIDE), lambda j, sides: (0, 0, sides[side] * steps + j)),
            ],
        ),
        out_shape=(
            jax.ShapeDtypeStruct((RANK, cols), F32),
            jax.ShapeDtypeStruct((1, rows, cols), BF16),
        ),
        input_output_aliases={5: 0, 6: 1} if partial else {},
        compiler_params=params(),
        cost_estimate=pl.CostEstimate(flops=2 * 160 * rows * cols // NC, bytes_accessed=6 * rows * cols, transcendentals=0),
        name="finish",
    )(sides, total, inverse, basis, grads, *partial)


def exchange(blocks, axis):
    return lax.all_to_all(blocks, axis, 0, 0, tiled=True)


def spread(block, axis):
    return exchange(jnp.broadcast_to(block[None], (lax.axis_size(axis),) + block.shape), axis)


def per_device(grads, q_prev):
    groups = lax.axis_size("dp")
    swap = [(0, 1), (1, 0)]

    own = lax.axis_index("c").astype(jnp.int32).reshape(1)
    shares, grads, sides = project(own, grads, q_prev, groups)
    shares = exchange(shares, "dp")
    away = lax.ppermute(term(1, sides, shares, grads), "c", swap)
    part = term(0, sides, shares, grads) + away
    part = jnp.sum(exchange(part, "x"), axis=0)
    tail = jnp.broadcast_to(part[-1], (NY, 1, SUB, LANE))
    part = jnp.concatenate([part[:-1].reshape(NY, TILES, SUB, LANE), tail], axis=1)
    part = jnp.sum(exchange(part, "y"), axis=0)
    inverse, basis = factor(part[TILES], shares, grads.shape[1])
    part = jnp.sum(spread(part[:TILES], "dp"), axis=0)

    total = spread(part, "y").reshape(NY * TILES, SUB, LANE)
    total = lax.all_gather(total, "x", axis=0)
    away = lax.ppermute(total, "c", swap)
    mine = finish(0, sides, total, inverse, basis, grads, groups)
    return tuple(finish(1, sides, away, inverse, basis, grads, groups, mine))


def solution(mesh):
    groups = mesh.devices.shape[1]
    fine = Mesh(mesh.devices.reshape(NY, NX, NC, groups), ("y", "x", "c", "dp"))
    split = P("dp", ("y", "x", "c"), None)
    return jax.shard_map(per_device, mesh=fine, in_specs=(split, P()), out_specs=(P(), split), check_vma=False)
```

time: 135 us -> 129 us (0.956)
  blocking collectives: 74.4 us -> 99.9 us
  starting transfers between devices: 30.5 us -> 14.8 us
  waiting for transfers between devices: 10.6 us -> 0.88 us
  local copies, waits for them, and re-layouts: 3.07 us -> 0.07 us
  Pallas kernels: 14.5 us -> 12.4 us
    all_to_all x4 -> x5, blocking collectives: 62.7 us -> 88.2 us  [exchange(): return lax.all_to_all(blocks, axis, 0, 0, tiled=True)]
    all_to_all x1 -> x0, starting transfers between devices: 15.7 us -> none  [exchange(): return lax.all_to_all(blocks, axis, 0, 0, tiled=True)]
    all_to_all x1 -> x0, waiting for transfers between devices: 10 us -> none  [exchange(): return lax.all_to_all(blocks, axis, 0, 0, tiled=True)]
    unnamed x6 -> x0, local copies, waits for them, and re-layouts: 3 us -> none
    pallas_call x1, Pallas kernels: 3.34 us -> 1.39 us  [factor(): pl.pallas_call(factor_kernel, out_shape=(jax.ShapeDtypeStruct((RANK, 2 *...]
  transfers between devices with their start and end apart: 3 -> 2, of which waited for: 2 -> 1; matrix products, arithmetic and copies ran while one was open for 0% -> 0% of each run, Pallas kernels for 6% -> 4%
where the time goes in v3:
time: 129 us
  blocking collectives  99.9 us (77%)
  starting transfers between devices  14.8 us (11%)
  Pallas kernels  12.4 us (10%)
    all_to_all x5, blocking collectives, exchange(): return lax.all_to_all(blocks, axis, 0, 0, tiled=True)  88.2 us
    all_gather x1, blocking collectives, per_device(): total = lax.all_gather(total, 'x', axis=0)  11.7 us
    ppermute x1, starting transfers between devices, per_device(): away = lax.ppermute(total, 'c', swap)  10 us
    pallas_call x2, Pallas kernels, finish(): pl.pallas_call(functools.partial(finish_kernel, groups), grid_spec=pltpu....  5.52 us
    ppermute x1, starting transfers between devices, per_device(): away = lax.ppermute(term(1, sides, shares, grads), 'c', swap)  4.8 us
    pallas_call x1, Pallas kernels, project(): pl.pallas_call(project_kernel, in_specs=[pl.BlockSpec(memory_space=pltpu....  3.01 us
  transfers between devices with their start and end apart: 2, of which 1 were waited for; matrix products, arithmetic and copies ran while one was open for 0% of the time, Pallas kernels for 4%

profile of v3, /device:TPU:1, one launch (start us, length us, event | category | flops | bytes accessed | tf_op | source)
XLA Modules:
  0.0 129.1 jit_solution(9262014342474151083)
XLA Ops:
  0.6 3.0 %project.1 = (f32[12,16,128]{2,1,0:T(8,128)S(1)}, bf16[1,64,14336]{2,1,0:T(8,128)(2,1)S(1)}, s32[2]{0:T(128)S(1)}) custom-call(s32[1]{0:T(128)} %bitcast.own_ref, bf16[1,64,14336]{2,1,0:T(8,128)(2,1)} %grads_ref.1, f32[32,14336]{1,0:T(8,128)} %q_ref.1), custom_call_target="tpu_custom_call" | custom-call | tf_op jit(solution)/shard_map/project/pallas_call | solution.py:81
  3.7 25.5 %all_to_all.25.shares_ref = f32[12,16,128]{2,1,0:T(8,128)S(1)} all-to-all(f32[12,16,128]{2,1,0:T(8,128)S(1)} %get-tuple-element.10), channel_id=1, replica_groups=mesh['y'=8,'x'=4,'c'=2,'dp'=12] {'dp'}, dimensions={0} | all-to-all | bytes 196608 | tf_op jit(solution)/shard_map/all_to_all | solution.py:236
  29.2 1.2 term.3
  30.4 4.8 %collective-permute-start = (f32[4,57,8,128]{3,2,1,0:T(8,128)S(1)}, f32[4,57,8,128]{3,2,1,0:T(8,128)S(1)}, u32[]{:S(2)}, u32[]{:S(2)}) collective-permute-start(f32[4,57,8,128]{3,2,1,0:T(8,128)S(1)} %term.3), channel_id=1, source_target_pairs={{0,12},{12,0},{1,13},{13,1},{2,14},{14,2},{3,15},{15,3},{4,16},{16... | collective-permute-start | bytes 2801672 | tf_op jit(solution)/shard_map/ppermute | solution.py:250
  35.2 1.2 term.2
  36.4 0.9 collective-permute-done
  37.3 0.1 add.3
  37.4 17.1 %all_to_all.26 = f32[4,57,8,128]{3,2,1,0:T(8,128)S(1)} all-to-all(f32[4,57,8,128]{3,2,1,0:T(8,128)S(1)} %add.3), channel_id=1, replica_groups=mesh['y'=8,'x'=4,'c'=2,'dp'=12] {'x'}, dimensions={0} | all-to-all | bytes 1867776 | tf_op jit(solution)/shard_map/all_to_all | solution.py:236
  54.6 0.1 reduce_sum.27
  54.7 16.1 %all_to_all.27 = f32[8,8,8,128]{3,2,1,0:T(8,128)S(1)} all-to-all(f32[8,8,8,128]{3,2,1,0:T(8,128)S(1)} %pad_maximum_fusion), channel_id=1, replica_groups=mesh['y'=8,'x'=4,'c'=2,'dp'=12] {'y'}, dimensions={0} | all-to-all | bytes 524288 | tf_op jit(solution)/shard_map/all_to_all | solution.py:236
  70.8 16.3 %all_to_all.28 = f32[12,7,8,128]{3,2,1,0:T(8,128)S(1)} all-to-all(f32[12,7,8,128]{3,2,1,0:T(8,128)S(1)} %broadcast_in_dim.7), channel_id=1, replica_groups=mesh['y'=8,'x'=4,'c'=2,'dp'=12] {'dp'}, dimensions={0} | all-to-all | bytes 688128 | tf_op jit(solution)/shard_map/all_to_all | solution.py:236
  87.2 13.2 %all_to_all.29 = f32[8,7,8,128]{3,2,1,0:T(8,128)S(1)} all-to-all(f32[8,7,8,128]{3,2,1,0:T(8,128)S(1)} %broadcast_in_dim.8), channel_id=1, replica_groups=mesh['y'=8,'x'=4,'c'=2,'dp'=12] {'y'}, dimensions={0} | all-to-all | bytes 458752 | tf_op jit(solution)/shard_map/all_to_all | solution.py:236
  100.4 11.7 %all_gather.3.total_ref = f32[4,56,8,128]{3,2,1,0:T(8,128)S(1)} all-gather(f32[1,56,8,128]{3,2,1,0:T(8,128)S(1)} %bitcast.8), channel_id=1, replica_groups=mesh['y'=8,'x'=4,'c'=2,'dp'=12] {'x'}, dimensions={0}, use_global_device_ids=true | all-gather | bytes 1146880 | tf_op jit(solution)/shard_map/all_gather | solution.py:260
  112.1 10.0 %collective-permute-start.1 = (f32[4,56,8,128]{3,2,1,0:T(8,128)S(1)}, f32[4,56,8,128]{3,2,1,0:T(8,128)S(1)}, u32[]{:S(2)}, u32[]{:S(2)}) collective-permute-start(f32[4,56,8,128]{3,2,1,0:T(8,128)S(1)} %all_gather.3.total_ref), channel_id=1, source_target_pairs={{0,12},{12,0},{1,13},{13,1},{2,14},{14,2},{3,15},{15,3},{4,16},{16... | collective-permute-start | bytes 2752520 | tf_op jit(solution)/shard_map/ppermute | solution.py:261
  122.1 1.4 %factor.1 = (bf16[32,256]{1,0:T(8,128)(2,1)S(1)}, bf16[64,128]{1,0:T(8,128)(2,1)S(1)}) custom-call(f32[8,128]{1,0:T(8,128)S(1)} %slice_bitcast_fusion.gram_ref, f32[12,16,128]{2,1,0:T(8,128)S(1)} %all_to_all.25.shares_ref), custom_call_target="tpu_custom_call" | custom-call | flops 4194304 | bytes 1048576 | tf_op jit(solution)/shard_map/factor/pallas_call | solution.py:177
  123.5 2.8 %finish.2 = (f32[32,14336]{1,0:T(8,128)}, bf16[1,64,14336]{2,1,0:T(8,128)(2,1)}) custom-call(s32[2]{0:T(128)S(1)} %get-tuple-element.9.sides_ref, f32[4,56,8,128]{3,2,1,0:T(8,128)S(1)} %all_gather.3.total_ref, bf16[32,256]{1,0:T(8,128)(2,1)S(1)} %get-tuple-element.12.inverse_ref, bf16[64,128]{1,0:T(8,128)(2,1)S(1)} %get-tuple-element.13.basis_ref, ...), custom_call_target="tpu_custom_call" | custom-call | flops 146800640 | bytes 5505024 | tf_op jit(solution)/shard_map/finish/pallas_call | solution.py:207
  126.3 0.0 collective-permute-done.1.total_ref
  126.3 2.8 %finish.3 = (f32[32,14336]{1,0:T(8,128)}, bf16[1,64,14336]{2,1,0:T(8,128)(2,1)}) custom-call(s32[2]{0:T(128)S(1)} %get-tuple-element.9.sides_ref, f32[4,56,8,128]{3,2,1,0:T(8,128)S(1)} %collective-permute-done.1.total_ref, bf16[32,256]{1,0:T(8,128)(2,1)S(1)} %get-tuple-element.12.inverse_ref, ...), custom_call_target="tpu_custom_call", output_to_operand_aliasing={{0}: (5, {}), {1}: (6, {})} | custom-call | flops 146800640 | bytes 5505024 | tf_op jit(solution)/shard_map/finish/pallas_call | solution.py:207
  (10 shorter events, 0.1 us)
Async XLA Ops:
  30.4 6.9 %collective-permute-start = (f32[4,57,8,128]{3,2,1,0:T(8,128)S(1)}, f32[4,57,8,128]{3,2,1,0:T(8,128)S(1)}, u32[]{:S(2)}, u32[]{:S(2)}) collective-permute-start(f32[4,57,8,128]{3,2,1,0:T(8,128)S(1)} %term.3), channel_id=1, source_target_pairs={{0,12},{12,0},{1,13},{13,1},{2,14},{14,2},{3,15},{15,3},{4,16},{16... | collective-permute-start | bytes 2801672 | tf_op jit(solution)/shard_map/ppermute | solution.py:250
  112.1 14.2 %collective-permute-start.1 = (f32[4,56,8,128]{3,2,1,0:T(8,128)S(1)}, f32[4,56,8,128]{3,2,1,0:T(8,128)S(1)}, u32[]{:S(2)}, u32[]{:S(2)}) collective-permute-start(f32[4,56,8,128]{3,2,1,0:T(8,128)S(1)} %all_gather.3.total_ref), channel_id=1, source_target_pairs={{0,12},{12,0},{1,13},{13,1},{2,14},{14,2},{3,15},{15,3},{4,16},{16... | collective-permute-start | bytes 2752520 | tf_op jit(solution)/shard_map/ppermute | solution.py:261

commit v4 on v3

--- a/solution.py
+++ b/solution.py
@@ -9,19 +9,15 @@
 
 HIGH = lax.Precision.HIGHEST
 F32, BF16 = jnp.float32, jnp.bfloat16
-NY, NX, NC = 8, 4, 2
+NY, NX, NC, NP = 8, 4, 2, 2
 SUB, LANE = 8, 128
 RANK = 32
-TILES = 7
-STEP = 28
+TILES = 4
+STEP = 14
 WIDE = STEP * LANE
 COPIES = 2
 AHEAD = 4
 VMEM = 24 * 1024 * 1024
-
-
-def params():
-    return pltpu.CompilerParams(vmem_limit_bytes=VMEM, dimension_semantics=("arbitrary",))
 
 
 def pieces(value, count):
@@ -112,15 +108,17 @@
     for x in range(NX):
         tile = jnp.where(slot == x, wide[x * SUB : (x + 1) * SUB], tile)
     for x in range(NX):
-        for t in range(tiles):
-            out_ref[x, t] = part[x * SUB : (x + 1) * SUB, t * LANE : (t + 1) * LANE]
-        out_ref[x, tiles] = tile
+        for p in range(NP):
+            for t in range(tiles):
+                cols = slice((p * tiles + t) * LANE, (p * tiles + t + 1) * LANE)
+                out_ref[x * NP + p, t] = part[x * SUB : (x + 1) * SUB, cols]
+            out_ref[x * NP + p, tiles] = tile
 
 
 def term(side, sides, shares, grads):
     rows, cols = grads.shape[1:]
     half = cols // NC
-    shape = (NX, half // LANE + 1, SUB, LANE)
+    shape = (NX * NP, half // NP // LANE + 1, SUB, LANE)
     return pl.pallas_call(
         term_kernel,
         grid_spec=pltpu.PrefetchScalarGridSpec(
@@ -133,14 +131,14 @@
             out_specs=pl.BlockSpec(shape, lambda j, sides: (0, 0, 0, 0)),
         ),
         out_shape=jax.ShapeDtypeStruct(shape, F32),
-        compiler_params=params(),
+        compiler_params=pltpu.CompilerParams(vmem_limit_bytes=VMEM),
         cost_estimate=pl.CostEstimate(flops=2 * 96 * rows * half, bytes_accessed=6 * rows * half, transcendentals=0),
         name="term",
     )(sides, shares, grads)
 
 
 def factor_kernel(gram_ref, shares_ref, inverse_ref, basis_ref):
-    tile = gram_ref[...]
+    tile = gram_ref[...] / shares_ref.shape[0]
     lane = lax.broadcasted_iota(jnp.int32, (RANK, LANE), 1)
     row = lax.broadcasted_iota(jnp.int32, (RANK, LANE), 0)
     work = jnp.concatenate([pltpu.roll(tile, (LANE - RANK * x) % LANE, 1) for x in range(NX)], axis=0)
@@ -186,48 +184,53 @@
     )(gram, shares)
 
 
-def finish_kernel(groups, sides_ref, total_ref, inverse_ref, basis_ref, grads_ref, *rest):
-    q_ref, resid_ref = rest[-2:]
-    total = jnp.concatenate(
-        [jnp.concatenate([total_ref[x, t] for x in range(NX)], axis=0) for t in range(STEP)], axis=1
-    )
-    one, two, three = pieces(total, 3)
-    stack = jnp.concatenate([one, two, one, three, two, one, one, one], axis=0)
-    q_new = dot(inverse_ref[...], stack, (1, 0)) / groups
-    q_ref[...] = q_new
-    high, low = pieces(q_new, 2)
-    approx = dot(basis_ref[...], jnp.concatenate([high, low, high, low], axis=0), (1, 0))
-    resid_ref[0] = (grads_ref[0].astype(F32) - approx).astype(BF16)
+def finish_kernel(groups, side, sides_ref, total_ref, inverse_ref, basis_ref, grads_ref, *rest):
+    q_ref, resid_ref, q_buf, resid_buf, sems = rest[-5:]
+    tiles = total_ref.shape[1] - 1
+    copies = []
+    for n in range(sems.shape[0]):
+        here = pl.ds(n * WIDE, WIDE)
+        there = pl.ds(pl.multiple_of(sides_ref[side] * q_buf.shape[1] + n * WIDE, LANE), WIDE)
+        columns = []
+        for t in range(n * STEP, (n + 1) * STEP):
+            parts = [total_ref[x * NP + t // tiles, t % tiles] for x in range(NX)]
+            columns.append(jnp.concatenate(parts, axis=0))
+        one, two, three = pieces(jnp.concatenate(columns, axis=1), 3)
+        stack = jnp.concatenate([one, two, one, three, two, one, one, one], axis=0)
+        q_new = dot(inverse_ref[...], stack, (1, 0)) / groups
+        q_buf[:, here] = q_new
+        copies.append(pltpu.make_async_copy(q_buf.at[:, here], q_ref.at[:, there], sems.at[n, 0]))
+        copies[-1].start()
+        high, low = pieces(q_new, 2)
+        approx = dot(basis_ref[...], jnp.concatenate([high, low, high, low], axis=0), (1, 0))
+        resid_buf[0, :, here] = (grads_ref[0, :, there].astype(F32) - approx).astype(BF16)
+        copies.append(pltpu.make_async_copy(resid_buf.at[:, :, here], resid_ref.at[:, :, there], sems.at[n, 1]))
+        copies[-1].start()
+    for copy in copies:
+        copy.wait()
 
 
 def finish(side, sides, total, inverse, basis, grads, groups, partial=()):
     rows, cols = grads.shape[1:]
-    steps = total.shape[1] // STEP
-    whole = lambda j, sides: (0, 0)
-    return pl.pallas_call(
-        functools.partial(finish_kernel, groups),
-        grid_spec=pltpu.PrefetchScalarGridSpec(
-            num_scalar_prefetch=1,
-            grid=(steps,),
-            in_specs=[
-                pl.BlockSpec((NX, STEP, SUB, LANE), lambda j, sides: (0, j, 0, 0)),
-                pl.BlockSpec(inverse.shape, whole),
-                pl.BlockSpec(basis.shape, whole),
-                pl.BlockSpec((1, rows, WIDE), lambda j, sides: (0, 0, sides[side] * steps + j)),
-            ]
-            + [pl.BlockSpec(memory_space=pl.ANY)] * len(partial),
-            out_specs=[
-                pl.BlockSpec((RANK, WIDE), lambda j, sides: (0, sides[side] * steps + j)),
-                pl.BlockSpec((1, rows, WIDE), lambda j, sides: (0, 0, sides[side] * steps + j)),
-            ],
-        ),
+    half = cols // NC
+    return pl.pallas_call(
+        functools.partial(finish_kernel, groups, side),
+        in_specs=[pl.BlockSpec(memory_space=pltpu.SMEM)]
+        + [pl.BlockSpec(memory_space=pltpu.VMEM)] * 4
+        + [pl.BlockSpec(memory_space=pl.ANY)] * len(partial),
+        out_specs=(pl.BlockSpec(memory_space=pl.ANY),) * 2,
         out_shape=(
             jax.ShapeDtypeStruct((RANK, cols), F32),
             jax.ShapeDtypeStruct((1, rows, cols), BF16),
         ),
+        scratch_shapes=[
+            pltpu.VMEM((RANK, half), F32),
+            pltpu.VMEM((1, rows, half), BF16),
+            pltpu.SemaphoreType.DMA((half // WIDE, 2)),
+        ],
         input_output_aliases={5: 0, 6: 1} if partial else {},
-        compiler_params=params(),
-        cost_estimate=pl.CostEstimate(flops=2 * 160 * rows * cols // NC, bytes_accessed=6 * rows * cols, transcendentals=0),
+        compiler_params=pltpu.CompilerParams(vmem_limit_bytes=VMEM),
+        cost_estimate=pl.CostEstimate(flops=2 * 160 * rows * half, bytes_accessed=6 * rows * half, transcendentals=0),
         name="finish",
     )(sides, total, inverse, basis, grads, *partial)
 
@@ -241,30 +244,30 @@
 
 
 def per_device(grads, q_prev):
-    groups = lax.axis_size("dp")
+    groups = lax.axis_size(("far", "near"))
     swap = [(0, 1), (1, 0)]
-
     own = lax.axis_index("c").astype(jnp.int32).reshape(1)
+
     shares, grads, sides = project(own, grads, q_prev, groups)
-    shares = exchange(shares, "dp")
+    shares = exchange(shares, ("far", "near"))
     away = lax.ppermute(term(1, sides, shares, grads), "c", swap)
     part = term(0, sides, shares, grads) + away
-    part = jnp.sum(exchange(part, "x"), axis=0)
-    tail = jnp.broadcast_to(part[-1], (NY, 1, SUB, LANE))
-    part = jnp.concatenate([part[:-1].reshape(NY, TILES, SUB, LANE), tail], axis=1)
-    part = jnp.sum(exchange(part, "y"), axis=0)
-    inverse, basis = factor(part[TILES], shares, grads.shape[1])
-    part = jnp.sum(spread(part[:TILES], "dp"), axis=0)
-
-    total = spread(part, "y").reshape(NY * TILES, SUB, LANE)
-    total = lax.all_gather(total, "x", axis=0)
+    used = part.shape[1]
+    part = jnp.sum(exchange(part, ("x", "near")), axis=0)
+    part = jnp.pad(part, ((0, NY * TILES - used), (0, 0), (0, 0)))
+    part = jnp.sum(exchange(part.reshape(NY, TILES, SUB, LANE), "y"), axis=0)
+    part = jnp.sum(spread(part, "far"), axis=0)
+
+    total = spread(part, "y").reshape(NY * TILES, SUB, LANE)[:used]
+    total = spread(total, ("x", "near"))
     away = lax.ppermute(total, "c", swap)
+    inverse, basis = factor(total[0, used - 1], shares, grads.shape[1])
     mine = finish(0, sides, total, inverse, basis, grads, groups)
     return tuple(finish(1, sides, away, inverse, basis, grads, groups, mine))
 
 
 def solution(mesh):
     groups = mesh.devices.shape[1]
-    fine = Mesh(mesh.devices.reshape(NY, NX, NC, groups), ("y", "x", "c", "dp"))
-    split = P("dp", ("y", "x", "c"), None)
+    fine = Mesh(mesh.devices.reshape(NY, NX, NC, groups // NP, NP), ("y", "x", "c", "far", "near"))
+    split = P(("far", "near"), ("y", "x", "c"), None)
     return jax.shard_map(per_device, mesh=fine, in_specs=(split, P()), out_specs=(P(), split), check_vma=False)

time: 129 us -> 121 us (0.938)
  blocking collectives: 99.9 us -> 92.4 us
    all_gather x1 -> x0, blocking collectives: 11.7 us -> none  [per_device(): total = lax.all_gather(total, 'x', axis=0)]
    all_to_all x5 -> x6, blocking collectives: 88.2 us -> 92.4 us  [exchange(): return lax.all_to_all(blocks, axis, 0, 0, tiled=True)]
where the time goes in v4:
time: 121 us; the launch traced here: 120 us
  blocking collectives  92.4 us (76%)
  starting transfers between devices  13.8 us (11%)
  Pallas kernels  12.2 us (10%)
    all_to_all x6, blocking collectives, exchange(): return lax.all_to_all(blocks, axis, 0, 0, tiled=True)  92.4 us
    ppermute x1, starting transfers between devices, per_device(): away = lax.ppermute(total, 'c', swap)  8.97 us
    pallas_call x2, Pallas kernels, finish(): pl.pallas_call(functools.partial(finish_kernel, groups, side), in_specs=[...  5.36 us
    ppermute x1, starting transfers between devices, per_device(): away = lax.ppermute(term(1, sides, shares, grads), 'c', swap)  4.8 us
    pallas_call x1, Pallas kernels, project(): pl.pallas_call(project_kernel, in_specs=[pl.BlockSpec(memory_space=pltpu....  3.01 us
    pallas_call x2, Pallas kernels, term(): pl.pallas_call(term_kernel, grid_spec=pltpu.PrefetchScalarGridSpec(num_sc...  2.44 us
  transfers between devices with their start and end apart: 2, of which 1 were waited for; matrix products, arithmetic and copies ran while one was open for 0% of the time, Pallas kernels for 4%

profile of v4, /device:TPU:1, one launch (start us, length us, event | category | flops | bytes accessed | tf_op | source)
XLA Modules:
  0.0 120.4 jit_solution(7872737475846101281)
XLA Ops:
  0.6 3.0 %project.1 = (f32[12,16,128]{2,1,0:T(8,128)S(1)}, bf16[1,64,14336]{2,1,0:T(8,128)(2,1)S(1)}, s32[2]{0:T(128)S(1)}) custom-call(s32[1]{0:T(128)} %bitcast.own_ref, bf16[1,64,14336]{2,1,0:T(8,128)(2,1)} %grads_ref.1, f32[32,14336]{1,0:T(8,128)} %q_ref.1), custom_call_target="tpu_custom_call" | custom-call | tf_op jit(solution)/shard_map/project/pallas_call | solution.py:77
  3.7 25.5 %all_to_all.30.shares_ref = f32[12,16,128]{2,1,0:T(8,128)S(1)} all-to-all(f32[12,16,128]{2,1,0:T(8,128)S(1)} %get-tuple-element.10), channel_id=1, replica_groups=mesh['y'=8,'x'=4,'c'=2,'far'=6,'near'=2] {'far','near'}, dimensions={0} | all-to-all | bytes 196608 | tf_op jit(solution)/shard_map/all_to_all | solution.py:239
  29.2 1.2 %term.3 = f32[8,29,8,128]{3,2,1,0:T(8,128)S(1)} custom-call(s32[2]{0:T(128)S(1)} %get-tuple-element.9.sides_ref, f32[12,16,128]{2,1,0:T(8,128)S(1)} %all_to_all.30.shares_ref, bf16[1,64,14336]{2,1,0:T(8,128)(2,1)S(1)} %get-tuple-element.11.grads_ref), custom_call_target="tpu_custom_call" | custom-call | flops 88080384 | bytes 2752512 | tf_op jit(solution)/shard_map/term/pallas_call | solution.py:122
  30.4 4.8 %collective-permute-start = (f32[8,29,8,128]{3,2,1,0:T(8,128)S(1)}, f32[8,29,8,128]{3,2,1,0:T(8,128)S(1)}, u32[]{:S(2)}, u32[]{:S(2)}) collective-permute-start(f32[8,29,8,128]{3,2,1,0:T(8,128)S(1)} %term.3), channel_id=1, source_target_pairs={{0,12},{12,0},{1,13},{13,1},{2,14},{14,2},{3,15},{15,3},{4,16},{16... | collective-permute-start | bytes 2850824 | tf_op jit(solution)/shard_map/ppermute | solution.py:253
  35.2 1.2 %term.2 = f32[8,29,8,128]{3,2,1,0:T(8,128)S(1)} custom-call(s32[2]{0:T(128)S(1)} %get-tuple-element.9.sides_ref, f32[12,16,128]{2,1,0:T(8,128)S(1)} %all_to_all.30.shares_ref, bf16[1,64,14336]{2,1,0:T(8,128)(2,1)S(1)} %get-tuple-element.11.grads_ref), custom_call_target="tpu_custom_call" | custom-call | flops 88080384 | bytes 2752512 | tf_op jit(solution)/shard_map/term/pallas_call | solution.py:122
  36.4 0.9 collective-permute-done
  37.3 0.1 add.5
  37.5 17.9 %all_to_all.31 = f32[8,29,8,128]{3,2,1,0:T(8,128)S(1)} all-to-all(f32[8,29,8,128]{3,2,1,0:T(8,128)S(1)} %add.5), channel_id=1, replica_groups=mesh['y'=8,'x'=4,'c'=2,'far'=6,'near'=2] {'x','near'}, dimensions={0} | all-to-all | bytes 1900544 | tf_op jit(solution)/shard_map/all_to_all | solution.py:239
  55.4 14.6 %all_to_all.32 = f32[8,4,8,128]{3,2,1,0:T(8,128)S(1)} all-to-all(f32[8,4,8,128]{3,2,1,0:T(8,128)S(1)} %bitcast.5), channel_id=1, replica_groups=mesh['y'=8,'x'=4,'c'=2,'far'=6,'near'=2] {'y'}, dimensions={0} | all-to-all | bytes 262144 | tf_op jit(solution)/shard_map/all_to_all | solution.py:239
  70.0 11.7 %all_to_all.33 = f32[6,4,8,128]{3,2,1,0:T(8,128)S(1)} all-to-all(f32[6,4,8,128]{3,2,1,0:T(8,128)S(1)} %broadcast_in_dim.6), channel_id=1, replica_groups=mesh['y'=8,'x'=4,'c'=2,'far'=6,'near'=2] {'far'}, dimensions={0} | all-to-all | bytes 196608 | tf_op jit(solution)/shard_map/all_to_all | solution.py:239
  81.8 10.3 %all_to_all.34 = f32[8,4,8,128]{3,2,1,0:T(8,128)S(1)} all-to-all(f32[8,4,8,128]{3,2,1,0:T(8,128)S(1)} %broadcast_in_dim.7), channel_id=1, replica_groups=mesh['y'=8,'x'=4,'c'=2,'far'=6,'near'=2] {'y'}, dimensions={0} | all-to-all | bytes 262144 | tf_op jit(solution)/shard_map/all_to_all | solution.py:239
  92.1 0.1 broadcast_in_dim.8
  92.2 12.4 %all_to_all.35.total_ref = f32[8,29,8,128]{3,2,1,0:T(8,128)S(1)} all-to-all(f32[8,29,8,128]{3,2,1,0:T(8,128)S(1)} %broadcast_in_dim.8), channel_id=1, replica_groups=mesh['y'=8,'x'=4,'c'=2,'far'=6,'near'=2] {'x','near'}, dimensions={0} | all-to-all | bytes 1900544 | tf_op jit(solution)/shard_map/all_to_all | solution.py:239
  104.6 9.0 %collective-permute-start.1 = (f32[8,29,8,128]{3,2,1,0:T(8,128)S(1)}, f32[8,29,8,128]{3,2,1,0:T(8,128)S(1)}, u32[]{:S(2)}, u32[]{:S(2)}) collective-permute-start(f32[8,29,8,128]{3,2,1,0:T(8,128)S(1)} %all_to_all.35.total_ref), channel_id=1, source_target_pairs={{0,12},{12,0},{1,13},{13,1},{2,14},{14,2},{3,15},{15,3},{4,16},{16... | collective-permute-start | bytes 2850824 | tf_op jit(solution)/shard_map/ppermute | solution.py:263
  113.6 1.4 %factor.1 = (bf16[32,256]{1,0:T(8,128)(2,1)S(1)}, bf16[64,128]{1,0:T(8,128)(2,1)S(1)}) custom-call(f32[8,128]{1,0:T(8,128)S(1)} %slice_bitcast_fusion.gram_ref, f32[12,16,128]{2,1,0:T(8,128)S(1)} %all_to_all.30.shares_ref), custom_call_target="tpu_custom_call" | custom-call | flops 4194304 | bytes 1048576 | tf_op jit(solution)/shard_map/factor/pallas_call | solution.py:175
  115.0 2.7 %finish.2 = (f32[32,14336]{1,0:T(8,128)}, bf16[1,64,14336]{2,1,0:T(8,128)(2,1)}) custom-call(s32[2]{0:T(128)S(1)} %get-tuple-element.9.sides_ref, f32[8,29,8,128]{3,2,1,0:T(8,128)S(1)} %all_to_all.35.total_ref, bf16[32,256]{1,0:T(8,128)(2,1)S(1)} %get-tuple-element.12.inverse_ref, bf16[64,128]{1,0:T(8,128)(2,1)S(1)} %get-tuple-element.13.basis_ref, ...), custom_call_target="tpu_custom_call" | custom-call | flops 146800640 | bytes 2752512 | tf_op jit(solution)/shard_map/finish/pallas_call | solution.py:216
  117.7 0.0 collective-permute-done.1.total_ref
  117.7 2.7 %finish.3 = (f32[32,14336]{1,0:T(8,128)}, bf16[1,64,14336]{2,1,0:T(8,128)(2,1)}) custom-call(s32[2]{0:T(128)S(1)} %get-tuple-element.9.sides_ref, f32[8,29,8,128]{3,2,1,0:T(8,128)S(1)} %collective-permute-done.1.total_ref, bf16[32,256]{1,0:T(8,128)(2,1)S(1)} %get-tuple-element.12.inverse_ref, ...), custom_call_target="tpu_custom_call", output_to_operand_aliasing={{0}: (5, {}), {1}: (6, {})} | custom-call | flops 146800640 | bytes 2752512 | tf_op jit(solution)/shard_map/finish/pallas_call | solution.py:216
  (8 shorter events, 0.1 us)
Async XLA Ops:
  30.4 6.9 %collective-permute-start = (f32[8,29,8,128]{3,2,1,0:T(8,128)S(1)}, f32[8,29,8,128]{3,2,1,0:T(8,128)S(1)}, u32[]{:S(2)}, u32[]{:S(2)}) collective-permute-start(f32[8,29,8,128]{3,2,1,0:T(8,128)S(1)} %term.3), channel_id=1, source_target_pairs={{0,12},{12,0},{1,13},{13,1},{2,14},{14,2},{3,15},{15,3},{4,16},{16... | collective-permute-start | bytes 2850824 | tf_op jit(solution)/shard_map/ppermute | solution.py:253
  104.6 13.1 %collective-permute-start.1 = (f32[8,29,8,128]{3,2,1,0:T(8,128)S(1)}, f32[8,29,8,128]{3,2,1,0:T(8,128)S(1)}, u32[]{:S(2)}, u32[]{:S(2)}) collective-permute-start(f32[8,29,8,128]{3,2,1,0:T(8,128)S(1)} %all_to_all.35.total_ref), channel_id=1, source_target_pairs={{0,12},{12,0},{1,13},{13,1},{2,14},{14,2},{3,15},{15,3},{4,16},{16... | collective-permute-start | bytes 2850824 | tf_op jit(solution)/shard_map/ppermute | solution.py:263

commit v5 on v4

--- a/solution.py
+++ b/solution.py
@@ -13,8 +13,6 @@
 SUB, LANE = 8, 128
 RANK = 32
 TILES = 4
-STEP = 14
-WIDE = STEP * LANE
 COPIES = 2
 AHEAD = 4
 VMEM = 24 * 1024 * 1024
@@ -63,10 +61,10 @@
         for copy in copies[n]:
             copy.wait()
         cols = pl.ds(n * wide, wide)
-        stack = jnp.concatenate(pieces(q_buf[:, cols], 3), axis=0)
+        stack = jnp.concatenate(pieces(q_buf[:, cols], 2), axis=0)
         part = dot(stack, grads_buf[0, :, cols], (1, 1))
         total = part if total is None else total + part
-    local = total[:RANK] + total[RANK : 2 * RANK] + total[2 * RANK :]
+    local = total[:RANK] + total[RANK:]
     packed = jnp.concatenate([local[: RANK // 2], local[RANK // 2 :]], axis=1)
     for g in range(out_ref.shape[0]):
         out_ref[g] = packed
@@ -96,13 +94,14 @@
     )(own, pltpu.with_memory_space_constraint(grads, pltpu.HBM), pltpu.with_memory_space_constraint(q_prev, pltpu.HBM))
 
 
-def term_kernel(sides_ref, shares_ref, grads_ref, out_ref):
+def term_kernel(side, sides_ref, shares_ref, grads_ref, out_ref):
     left = left_of(shares_ref)
-    stack = jnp.concatenate(pieces(left, 3), axis=0)
-    part = dot(stack, grads_ref[0], (1, 0))
-    part = part[:RANK] + part[RANK : 2 * RANK] + part[2 * RANK :]
+    stack = jnp.concatenate(pieces(left, 2), axis=0)
+    half = grads_ref.shape[2] // NC
+    part = dot(stack, grads_ref[0, :, half_of(side, sides_ref, half)], (1, 0))
+    part = part[:RANK] + part[RANK:]
     tiles = out_ref.shape[1] - 1
-    wide = dot(left, jnp.concatenate([left] * NX, axis=0), (1, 1), HIGH)
+    wide = dot(left, jnp.concatenate([left] * NX, axis=0), (1, 1), HIGH) / shares_ref.shape[0]
     slot = lax.broadcasted_iota(jnp.int32, (SUB, LANE), 1) // RANK
     tile = jnp.zeros((SUB, LANE), F32)
     for x in range(NX):
@@ -120,16 +119,9 @@
     half = cols // NC
     shape = (NX * NP, half // NP // LANE + 1, SUB, LANE)
     return pl.pallas_call(
-        term_kernel,
-        grid_spec=pltpu.PrefetchScalarGridSpec(
-            num_scalar_prefetch=1,
-            grid=(1,),
-            in_specs=[
-                pl.BlockSpec(shares.shape, lambda j, sides: (0, 0, 0)),
-                pl.BlockSpec((1, rows, half), lambda j, sides: (0, 0, sides[side])),
-            ],
-            out_specs=pl.BlockSpec(shape, lambda j, sides: (0, 0, 0, 0)),
-        ),
+        functools.partial(term_kernel, side),
+        in_specs=[pl.BlockSpec(memory_space=pltpu.SMEM)] + [pl.BlockSpec(memory_space=pltpu.VMEM)] * 2,
+        out_specs=pl.BlockSpec(memory_space=pltpu.VMEM),
         out_shape=jax.ShapeDtypeStruct(shape, F32),
         compiler_params=pltpu.CompilerParams(vmem_limit_bytes=VMEM),
         cost_estimate=pl.CostEstimate(flops=2 * 96 * rows * half, bytes_accessed=6 * rows * half, transcendentals=0),
@@ -138,7 +130,7 @@
 
 
 def factor_kernel(gram_ref, shares_ref, inverse_ref, basis_ref):
-    tile = gram_ref[...] / shares_ref.shape[0]
+    tile = gram_ref[...]
     lane = lax.broadcasted_iota(jnp.int32, (RANK, LANE), 1)
     row = lax.broadcasted_iota(jnp.int32, (RANK, LANE), 0)
     work = jnp.concatenate([pltpu.roll(tile, (LANE - RANK * x) % LANE, 1) for x in range(NX)], axis=0)
@@ -158,13 +150,10 @@
     pivots = jnp.sum(jnp.where(lane == row, work, 0.0), axis=1, keepdims=True)
     work = work * (1.0 / jnp.sqrt(pivots))
     inverse = jnp.where(lane < RANK, pltpu.roll(work, LANE - RANK, 1), 0.0)
-    one, two, three = [part.astype(F32) for part in pieces(inverse, 3)]
-
-    def at(value, slot):
-        return pltpu.roll(value, RANK * slot, 1) if slot else value
-
-    inverse_ref[:, :LANE] = (at(one, 0) + at(one, 1) + at(two, 2) + at(one, 3)).astype(BF16)
-    inverse_ref[:, LANE:] = (at(two, 0) + at(three, 1)).astype(BF16)
+    one, two = [part.astype(F32) for part in pieces(inverse, 2)]
+    one = one + pltpu.roll(one, RANK, 1)
+    two = two + pltpu.roll(two, RANK, 1)
+    inverse_ref[...] = (one + pltpu.roll(two, 2 * RANK, 1)).astype(BF16)
     basis = dot(left_of(shares_ref), jnp.concatenate([inverse[:, :RANK]] * 4, axis=0), (0, 1), HIGH)
     high = basis.astype(BF16).astype(F32)
     wide = lax.broadcasted_iota(jnp.int32, basis.shape, 1)
@@ -175,7 +164,7 @@
     return pl.pallas_call(
         factor_kernel,
         out_shape=(
-            jax.ShapeDtypeStruct((RANK, 2 * LANE), BF16),
+            jax.ShapeDtypeStruct((RANK, LANE), BF16),
             jax.ShapeDtypeStruct((rows, LANE), BF16),
         ),
         compiler_params=pltpu.CompilerParams(vmem_limit_bytes=VMEM),
@@ -184,40 +173,75 @@
     )(gram, shares)
 
 
-def finish_kernel(groups, side, sides_ref, total_ref, inverse_ref, basis_ref, grads_ref, *rest):
-    q_ref, resid_ref, q_buf, resid_buf, sems = rest[-5:]
+def solve(total_ref, inverse_ref, groups):
     tiles = total_ref.shape[1] - 1
-    copies = []
-    for n in range(sems.shape[0]):
-        here = pl.ds(n * WIDE, WIDE)
-        there = pl.ds(pl.multiple_of(sides_ref[side] * q_buf.shape[1] + n * WIDE, LANE), WIDE)
-        columns = []
-        for t in range(n * STEP, (n + 1) * STEP):
-            parts = [total_ref[x * NP + t // tiles, t % tiles] for x in range(NX)]
-            columns.append(jnp.concatenate(parts, axis=0))
-        one, two, three = pieces(jnp.concatenate(columns, axis=1), 3)
-        stack = jnp.concatenate([one, two, one, three, two, one, one, one], axis=0)
-        q_new = dot(inverse_ref[...], stack, (1, 0)) / groups
-        q_buf[:, here] = q_new
-        copies.append(pltpu.make_async_copy(q_buf.at[:, here], q_ref.at[:, there], sems.at[n, 0]))
-        copies[-1].start()
-        high, low = pieces(q_new, 2)
-        approx = dot(basis_ref[...], jnp.concatenate([high, low, high, low], axis=0), (1, 0))
-        resid_buf[0, :, here] = (grads_ref[0, :, there].astype(F32) - approx).astype(BF16)
-        copies.append(pltpu.make_async_copy(resid_buf.at[:, :, here], resid_ref.at[:, :, there], sems.at[n, 1]))
-        copies[-1].start()
+    columns = []
+    for t in range(NP * tiles):
+        parts = [total_ref[x * NP + t // tiles, t % tiles] for x in range(NX)]
+        columns.append(jnp.concatenate(parts, axis=0))
+    one, two = pieces(jnp.concatenate(columns, axis=1), 2)
+    return dot(inverse_ref[...], jnp.concatenate([one, two, one, two], axis=0), (1, 0)) / groups
+
+
+def residual(q_new, basis_ref, grads):
+    high, low = pieces(q_new, 2)
+    approx = dot(basis_ref[...], jnp.concatenate([high, low, high, low], axis=0), (1, 0))
+    return (grads.astype(F32) - approx).astype(BF16)
+
+
+def half_of(side, sides_ref, half):
+    return pl.ds(pl.multiple_of(sides_ref[side] * half, LANE), half)
+
+
+def mine_kernel(groups, sides_ref, total_ref, inverse_ref, basis_ref, grads_ref, q_ref, resid_ref):
+    q_new = solve(total_ref, inverse_ref, groups)
+    q_ref[...] = q_new
+    resid_ref[0] = residual(q_new, basis_ref, grads_ref[0, :, half_of(0, sides_ref, q_ref.shape[1])])
+
+
+def mine(sides, total, inverse, basis, grads, groups):
+    rows, cols = grads.shape[1:]
+    half = cols // NC
+    return pl.pallas_call(
+        functools.partial(mine_kernel, groups),
+        in_specs=[pl.BlockSpec(memory_space=pltpu.SMEM)] + [pl.BlockSpec(memory_space=pltpu.VMEM)] * 4,
+        out_specs=(pl.BlockSpec(memory_space=pltpu.VMEM),) * 2,
+        out_shape=(pltpu.VMEM((RANK, half), F32), pltpu.VMEM((1, rows, half), BF16)),
+        compiler_params=pltpu.CompilerParams(vmem_limit_bytes=VMEM),
+        cost_estimate=pl.CostEstimate(flops=2 * 160 * rows * half, bytes_accessed=6 * rows * half, transcendentals=0),
+        name="mine",
+    )(sides, total, inverse, basis, grads)
+
+
+def finish_kernel(
+    groups, sides_ref, total_ref, inverse_ref, basis_ref, grads_ref, mine_q_ref, mine_resid_ref,
+    q_ref, resid_ref, q_buf, resid_buf, sems,
+):
+    half = q_buf.shape[1]
+    here, there = half_of(0, sides_ref, half), half_of(1, sides_ref, half)
+    copies = [
+        pltpu.make_async_copy(mine_q_ref, q_ref.at[:, here], sems.at[0]),
+        pltpu.make_async_copy(mine_resid_ref, resid_ref.at[:, :, here], sems.at[1]),
+        pltpu.make_async_copy(q_buf, q_ref.at[:, there], sems.at[2]),
+        pltpu.make_async_copy(resid_buf, resid_ref.at[:, :, there], sems.at[3]),
+    ]
+    copies[0].start()
+    copies[1].start()
+    q_new = solve(total_ref, inverse_ref, groups)
+    q_buf[...] = q_new
+    copies[2].start()
+    resid_buf[0] = residual(q_new, basis_ref, grads_ref[0, :, there])
+    copies[3].start()
     for copy in copies:
         copy.wait()
 
 
-def finish(side, sides, total, inverse, basis, grads, groups, partial=()):
+def finish(sides, total, inverse, basis, grads, groups, done):
     rows, cols = grads.shape[1:]
     half = cols // NC
     return pl.pallas_call(
-        functools.partial(finish_kernel, groups, side),
-        in_specs=[pl.BlockSpec(memory_space=pltpu.SMEM)]
-        + [pl.BlockSpec(memory_space=pltpu.VMEM)] * 4
-        + [pl.BlockSpec(memory_space=pl.ANY)] * len(partial),
+        functools.partial(finish_kernel, groups),
+        in_specs=[pl.BlockSpec(memory_space=pltpu.SMEM)] + [pl.BlockSpec(memory_space=pltpu.VMEM)] * 6,
         out_specs=(pl.BlockSpec(memory_space=pl.ANY),) * 2,
         out_shape=(
             jax.ShapeDtypeStruct((RANK, cols), F32),
@@ -226,13 +250,11 @@
         scratch_shapes=[
             pltpu.VMEM((RANK, half), F32),
             pltpu.VMEM((1, rows, half), BF16),
-            pltpu.SemaphoreType.DMA((half // WIDE, 2)),
+            pltpu.SemaphoreType.DMA((4,)),
         ],
-        input_output_aliases={5: 0, 6: 1} if partial else {},
-        compiler_params=pltpu.CompilerParams(vmem_limit_bytes=VMEM),
-        cost_estimate=pl.CostEstimate(flops=2 * 160 * rows * half, bytes_accessed=6 * rows * half, transcendentals=0),
+        compiler_params=pltpu.CompilerParams(vmem_limit_bytes=VMEM),
         name="finish",
-    )(sides, total, inverse, basis, grads, *partial)
+    )(sides, total, inverse, basis, grads, *done)
 
 
 def exchange(blocks, axis):
@@ -262,8 +284,8 @@
     total = spread(total, ("x", "near"))
     away = lax.ppermute(total, "c", swap)
     inverse, basis = factor(total[0, used - 1], shares, grads.shape[1])
-    mine = finish(0, sides, total, inverse, basis, grads, groups)
-    return tuple(finish(1, sides, away, inverse, basis, grads, groups, mine))
+    done = mine(sides, total, inverse, basis, grads, groups)
+    return tuple(finish(sides, away, inverse, basis, grads, groups, done))
 
 
 def solution(mesh):

time: 121 us -> 119 us (0.983)
  Pallas kernels: 12.2 us -> 10.4 us
    pallas_call x5, Pallas kernels: 9.2 us -> 7.65 us  [the longest x1 2.9 us: finish(): pl.pallas_call(functools.partial(finish_kernel, groups), in_specs=[pl.Blo...]
  transfers between devices with their start and end apart: 2 -> 2, of which waited for: 1 -> 1; matrix products, arithmetic and copies ran while one was open for 0% -> 0% of each run, Pallas kernels for 4% -> 3%
where the time goes in v5:
time: 119 us
  blocking collectives  92.4 us (78%)
  starting transfers between devices  13.8 us (12%)
  Pallas kernels  10.4 us (9%)
    all_to_all x6, blocking collectives, exchange(): return lax.all_to_all(blocks, axis, 0, 0, tiled=True)  92.4 us
    ppermute x1, starting transfers between devices, per_device(): away = lax.ppermute(total, 'c', swap)  8.97 us
    ppermute x1, starting transfers between devices, per_device(): away = lax.ppermute(term(1, sides, shares, grads), 'c', swap)  4.81 us
    pallas_call x1, Pallas kernels, finish(): pl.pallas_call(functools.partial(finish_kernel, groups), in_specs=[pl.Blo...  2.9 us
    pallas_call x1, Pallas kernels, project(): pl.pallas_call(project_kernel, in_specs=[pl.BlockSpec(memory_space=pltpu....  2.78 us
  transfers between devices with their start and end apart: 2, of which 1 were waited for; matrix products, arithmetic and copies ran while one was open for 0% of the time, Pallas kernels for 3%

profile of v5, /device:TPU:1, one launch (start us, length us, event | category | flops | bytes accessed | tf_op | source)
XLA Modules:
  0.0 118.7 jit_solution(2864947584605976315)
XLA Ops:
  0.6 2.8 %project.1 = (f32[12,16,128]{2,1,0:T(8,128)S(1)}, bf16[1,64,14336]{2,1,0:T(8,128)(2,1)S(1)}, s32[2]{0:T(128)S(1)}) custom-call(s32[1]{0:T(128)} %bitcast.own_ref, bf16[1,64,14336]{2,1,0:T(8,128)(2,1)} %grads_ref.1, f32[32,14336]{1,0:T(8,128)} %q_ref.1), custom_call_target="tpu_custom_call" | custom-call | tf_op jit(solution)/shard_map/project/pallas_call | solution.py:75
  3.4 25.5 %all_to_all.30.shares_ref = f32[12,16,128]{2,1,0:T(8,128)S(1)} all-to-all(f32[12,16,128]{2,1,0:T(8,128)S(1)} %get-tuple-element.10), channel_id=1, replica_groups=mesh['y'=8,'x'=4,'c'=2,'far'=6,'near'=2] {'far','near'}, dimensions={0} | all-to-all | bytes 196608 | tf_op jit(solution)/shard_map/all_to_all | solution.py:261
  28.9 1.1 term.3
  30.0 4.8 %collective-permute-start = (f32[8,29,8,128]{3,2,1,0:T(8,128)S(1)}, f32[8,29,8,128]{3,2,1,0:T(8,128)S(1)}, u32[]{:S(2)}, u32[]{:S(2)}) collective-permute-start(f32[8,29,8,128]{3,2,1,0:T(8,128)S(1)} %term.3), channel_id=1, source_target_pairs={{0,12},{12,0},{1,13},{13,1},{2,14},{14,2},{3,15},{15,3},{4,16},{16... | collective-permute-start | bytes 2850824 | tf_op jit(solution)/shard_map/ppermute | solution.py:275
  34.9 1.1 term.2
  35.9 1.0 collective-permute-done
  37.0 0.1 add.5
  37.1 17.9 %all_to_all.31 = f32[8,29,8,128]{3,2,1,0:T(8,128)S(1)} all-to-all(f32[8,29,8,128]{3,2,1,0:T(8,128)S(1)} %add.5), channel_id=1, replica_groups=mesh['y'=8,'x'=4,'c'=2,'far'=6,'near'=2] {'x','near'}, dimensions={0} | all-to-all | bytes 1900544 | tf_op jit(solution)/shard_map/all_to_all | solution.py:261
  55.1 14.6 %all_to_all.32 = f32[8,4,8,128]{3,2,1,0:T(8,128)S(1)} all-to-all(f32[8,4,8,128]{3,2,1,0:T(8,128)S(1)} %bitcast.5), channel_id=1, replica_groups=mesh['y'=8,'x'=4,'c'=2,'far'=6,'near'=2] {'y'}, dimensions={0} | all-to-all | bytes 262144 | tf_op jit(solution)/shard_map/all_to_all | solution.py:261
  69.7 11.7 %all_to_all.33 = f32[6,4,8,128]{3,2,1,0:T(8,128)S(1)} all-to-all(f32[6,4,8,128]{3,2,1,0:T(8,128)S(1)} %broadcast_in_dim.6), channel_id=1, replica_groups=mesh['y'=8,'x'=4,'c'=2,'far'=6,'near'=2] {'far'}, dimensions={0} | all-to-all | bytes 196608 | tf_op jit(solution)/shard_map/all_to_all | solution.py:261
  81.4 10.3 %all_to_all.34 = f32[8,4,8,128]{3,2,1,0:T(8,128)S(1)} all-to-all(f32[8,4,8,128]{3,2,1,0:T(8,128)S(1)} %broadcast_in_dim.7), channel_id=1, replica_groups=mesh['y'=8,'x'=4,'c'=2,'far'=6,'near'=2] {'y'}, dimensions={0} | all-to-all | bytes 262144 | tf_op jit(solution)/shard_map/all_to_all | solution.py:261
  91.7 0.1 broadcast_in_dim.8
  91.8 12.4 %all_to_all.35.total_ref = f32[8,29,8,128]{3,2,1,0:T(8,128)S(1)} all-to-all(f32[8,29,8,128]{3,2,1,0:T(8,128)S(1)} %broadcast_in_dim.8), channel_id=1, replica_groups=mesh['y'=8,'x'=4,'c'=2,'far'=6,'near'=2] {'x','near'}, dimensions={0} | all-to-all | bytes 1900544 | tf_op jit(solution)/shard_map/all_to_all | solution.py:261
  104.2 9.0 %collective-permute-start.1 = (f32[8,29,8,128]{3,2,1,0:T(8,128)S(1)}, f32[8,29,8,128]{3,2,1,0:T(8,128)S(1)}, u32[]{:S(2)}, u32[]{:S(2)}) collective-permute-start(f32[8,29,8,128]{3,2,1,0:T(8,128)S(1)} %all_to_all.35.total_ref), channel_id=1, source_target_pairs={{0,12},{12,0},{1,13},{13,1},{2,14},{14,2},{3,15},{15,3},{4,16},{16... | collective-permute-start | bytes 2850824 | tf_op jit(solution)/shard_map/ppermute | solution.py:285
  113.2 1.4 %factor.1 = (bf16[32,128]{1,0:T(8,128)(2,1)S(1)}, bf16[64,128]{1,0:T(8,128)(2,1)S(1)}) custom-call(f32[8,128]{1,0:T(8,128)S(1)} %slice_bitcast_fusion.gram_ref, f32[12,16,128]{2,1,0:T(8,128)S(1)} %all_to_all.30.shares_ref), custom_call_target="tpu_custom_call" | custom-call | flops 4194304 | bytes 1048576 | tf_op jit(solution)/shard_map/factor/pallas_call | solution.py:164
  114.6 1.2 mine.1
  115.8 0.0 collective-permute-done.1.total_ref
  115.8 2.9 %finish.1 = (f32[32,14336]{1,0:T(8,128)}, bf16[1,64,14336]{2,1,0:T(8,128)(2,1)}) custom-call(s32[2]{0:T(128)S(1)} %get-tuple-element.9.sides_ref, f32[8,29,8,128]{3,2,1,0:T(8,128)S(1)} %collective-permute-done.1.total_ref, bf16[32,128]{1,0:T(8,128)(2,1)S(1)} %get-tuple-element.12.inverse_ref, bf16[64,128]{1,0:T(8,128)(2,1)S(1)} %get-tuple-element.13.basis_ref, ...), custom_call_target="tpu_custom_call" | custom-call | tf_op jit(solution)/shard_map/finish/pallas_call | solution.py:242
  (8 shorter events, 0.1 us)
Async XLA Ops:
  30.0 6.9 %collective-permute-start = (f32[8,29,8,128]{3,2,1,0:T(8,128)S(1)}, f32[8,29,8,128]{3,2,1,0:T(8,128)S(1)}, u32[]{:S(2)}, u32[]{:S(2)}) collective-permute-start(f32[8,29,8,128]{3,2,1,0:T(8,128)S(1)} %term.3), channel_id=1, source_target_pairs={{0,12},{12,0},{1,13},{13,1},{2,14},{14,2},{3,15},{15,3},{4,16},{16... | collective-permute-start | bytes 2850824 | tf_op jit(solution)/shard_map/ppermute | solution.py:275
  104.2 11.6 %collective-permute-start.1 = (f32[8,29,8,128]{3,2,1,0:T(8,128)S(1)}, f32[8,29,8,128]{3,2,1,0:T(8,128)S(1)}, u32[]{:S(2)}, u32[]{:S(2)}) collective-permute-start(f32[8,29,8,128]{3,2,1,0:T(8,128)S(1)} %all_to_all.35.total_ref), channel_id=1, source_target_pairs={{0,12},{12,0},{1,13},{13,1},{2,14},{14,2},{3,15},{15,3},{4,16},{16... | collective-permute-start | bytes 2850824 | tf_op jit(solution)/shard_map/ppermute | solution.py:285

commit v6 on v5

--- a/solution.py
+++ b/solution.py
@@ -9,7 +9,8 @@
 
 HIGH = lax.Precision.HIGHEST
 F32, BF16 = jnp.float32, jnp.bfloat16
-NY, NX, NC, NP = 8, 4, 2, 2
+NY, NX, NC, PAIR = 4, 4, 2, 2
+NP = PAIR * PAIR
 SUB, LANE = 8, 128
 RANK = 32
 TILES = 4
@@ -275,13 +276,13 @@
     away = lax.ppermute(term(1, sides, shares, grads), "c", swap)
     part = term(0, sides, shares, grads) + away
     used = part.shape[1]
-    part = jnp.sum(exchange(part, ("x", "near")), axis=0)
+    part = jnp.sum(exchange(part, ("x", "near", "side")), axis=0)
     part = jnp.pad(part, ((0, NY * TILES - used), (0, 0), (0, 0)))
     part = jnp.sum(exchange(part.reshape(NY, TILES, SUB, LANE), "y"), axis=0)
     part = jnp.sum(spread(part, "far"), axis=0)
 
     total = spread(part, "y").reshape(NY * TILES, SUB, LANE)[:used]
-    total = spread(total, ("x", "near"))
+    total = spread(total, ("x", "near", "side"))
     away = lax.ppermute(total, "c", swap)
     inverse, basis = factor(total[0, used - 1], shares, grads.shape[1])
     done = mine(sides, total, inverse, basis, grads, groups)
@@ -290,6 +291,7 @@
 
 def solution(mesh):
     groups = mesh.devices.shape[1]
-    fine = Mesh(mesh.devices.reshape(NY, NX, NC, groups // NP, NP), ("y", "x", "c", "far", "near"))
-    split = P(("far", "near"), ("y", "x", "c"), None)
+    shape = (NY, PAIR, NX, NC, groups // PAIR, PAIR)
+    fine = Mesh(mesh.devices.reshape(shape), ("y", "side", "x", "c", "far", "near"))
+    split = P(("far", "near"), ("y", "side", "x", "c"), None)
     return jax.shard_map(per_device, mesh=fine, in_specs=(split, P()), out_specs=(P(), split), check_vma=False)

time: 119 us -> 119 us (level)
  no operation moved by 1% of the time
where the time goes in v6:
time: 119 us
  blocking collectives  92.9 us (78%)
  starting transfers between devices  13.7 us (12%)
  Pallas kernels  10.4 us (9%)
    all_to_all x6, blocking collectives, exchange(): return lax.all_to_all(blocks, axis, 0, 0, tiled=True)  92.9 us
    ppermute x1, starting transfers between devices, per_device(): away = lax.ppermute(total, 'c', swap)  8.89 us
    ppermute x1, starting transfers between devices, per_device(): away = lax.ppermute(term(1, sides, shares, grads), 'c', swap)  4.81 us
    pallas_call x1, Pallas kernels, finish(): pl.pallas_call(functools.partial(finish_kernel, groups), in_specs=[pl.Blo...  2.89 us
    pallas_call x1, Pallas kernels, project(): pl.pallas_call(project_kernel, in_specs=[pl.BlockSpec(memory_space=pltpu....  2.78 us
  transfers between devices with their start and end apart: 2, of which 1 were waited for; matrix products, arithmetic and copies ran while one was open for 0% of the time, Pallas kernels for 3%

profile of v6, /device:TPU:1, one launch (start us, length us, event | category | flops | bytes accessed | tf_op | source)
XLA Modules:
  0.0 119.1 jit_solution(11756270425453992343)
XLA Ops:
  0.6 2.8 %project.1 = (f32[12,16,128]{2,1,0:T(8,128)S(1)}, bf16[1,64,14336]{2,1,0:T(8,128)(2,1)S(1)}, s32[2]{0:T(128)S(1)}) custom-call(s32[1]{0:T(128)} %bitcast.own_ref, bf16[1,64,14336]{2,1,0:T(8,128)(2,1)} %grads_ref.1, f32[32,14336]{1,0:T(8,128)} %q_ref.1), custom_call_target="tpu_custom_call" | custom-call | tf_op jit(solution)/shard_map/project/pallas_call | solution.py:76
  3.4 25.5 %all_to_all.30.shares_ref = f32[12,16,128]{2,1,0:T(8,128)S(1)} all-to-all(f32[12,16,128]{2,1,0:T(8,128)S(1)} %get-tuple-element.10), channel_id=1, replica_groups=mesh['y'=4,'side'=2,'x'=4,'c'=2,'far'=6,'near'=2] {'far','near'}, dimensions={0} | all-to-all | bytes 196608 | tf_op jit(solution)/shard_map/all_to_all | solution.py:262
  28.9 1.1 term.3
  30.1 4.8 %collective-permute-start = (f32[16,15,8,128]{3,2,1,0:T(8,128)S(1)}, f32[16,15,8,128]{3,2,1,0:T(8,128)S(1)}, u32[]{:S(2)}, u32[]{:S(2)}) collective-permute-start(f32[16,15,8,128]{3,2,1,0:T(8,128)S(1)} %term.3), channel_id=1, source_target_pairs={{0,12},{12,0},{1,13},{13,1},{2,14},{14,2},{3,15},{15,3},{4,16},{16... | collective-permute-start | bytes 2949128 | tf_op jit(solution)/shard_map/ppermute | solution.py:276
  34.9 1.1 term.2
  36.0 1.1 collective-permute-done
  37.0 0.1 add.5
  37.2 19.0 %all_to_all.31 = f32[16,15,8,128]{3,2,1,0:T(8,128)S(1)} all-to-all(f32[16,15,8,128]{3,2,1,0:T(8,128)S(1)} %add.5), channel_id=1, replica_groups=mesh['y'=4,'side'=2,'x'=4,'c'=2,'far'=6,'near'=2] {'x','near','side'}, dimensions={0} | all-to-all | bytes 1966080 | tf_op jit(solution)/shard_map/all_to_all | solution.py:262
  56.1 0.1 reduce_sum.27
  56.2 12.6 %all_to_all.32 = f32[4,4,8,128]{3,2,1,0:T(8,128)S(1)} all-to-all(f32[4,4,8,128]{3,2,1,0:T(8,128)S(1)} %bitcast.5), channel_id=1, replica_groups=mesh['y'=4,'side'=2,'x'=4,'c'=2,'far'=6,'near'=2] {'y'}, dimensions={0} | all-to-all | bytes 131072 | tf_op jit(solution)/shard_map/all_to_all | solution.py:262
  68.8 11.8 %all_to_all.33 = f32[6,4,8,128]{3,2,1,0:T(8,128)S(1)} all-to-all(f32[6,4,8,128]{3,2,1,0:T(8,128)S(1)} %broadcast_in_dim.6), channel_id=1, replica_groups=mesh['y'=4,'side'=2,'x'=4,'c'=2,'far'=6,'near'=2] {'far'}, dimensions={0} | all-to-all | bytes 196608 | tf_op jit(solution)/shard_map/all_to_all | solution.py:262
  80.6 9.2 %all_to_all.34 = f32[4,4,8,128]{3,2,1,0:T(8,128)S(1)} all-to-all(f32[4,4,8,128]{3,2,1,0:T(8,128)S(1)} %broadcast_in_dim.7), channel_id=1, replica_groups=mesh['y'=4,'side'=2,'x'=4,'c'=2,'far'=6,'near'=2] {'y'}, dimensions={0} | all-to-all | bytes 131072 | tf_op jit(solution)/shard_map/all_to_all | solution.py:262
  89.9 0.1 broadcast_in_dim.8
  90.0 14.7 %all_to_all.35.total_ref = f32[16,15,8,128]{3,2,1,0:T(8,128)S(1)} all-to-all(f32[16,15,8,128]{3,2,1,0:T(8,128)S(1)} %broadcast_in_dim.8), channel_id=1, replica_groups=mesh['y'=4,'side'=2,'x'=4,'c'=2,'far'=6,'near'=2] {'x','near','side'}, dimensions={0} | all-to-all | bytes 1966080 | tf_op jit(solution)/shard_map/all_to_all | solution.py:262
  104.7 8.9 %collective-permute-start.1 = (f32[16,15,8,128]{3,2,1,0:T(8,128)S(1)}, f32[16,15,8,128]{3,2,1,0:T(8,128)S(1)}, u32[]{:S(2)}, u32[]{:S(2)}) collective-permute-start(f32[16,15,8,128]{3,2,1,0:T(8,128)S(1)} %all_to_all.35.total_ref), channel_id=1, source_target_pairs={{0,12},{12,0},{1,13},{13,1},{2,14},{14,2},{3,15},{15,3},{4,16},{16... | collective-permute-start | bytes 2949128 | tf_op jit(solution)/shard_map/ppermute | solution.py:286
  113.6 1.4 %factor.1 = (bf16[32,128]{1,0:T(8,128)(2,1)S(1)}, bf16[64,128]{1,0:T(8,128)(2,1)S(1)}) custom-call(f32[8,128]{1,0:T(8,128)S(1)} %slice_bitcast_fusion.gram_ref, f32[12,16,128]{2,1,0:T(8,128)S(1)} %all_to_all.30.shares_ref), custom_call_target="tpu_custom_call" | custom-call | flops 4194304 | bytes 1048576 | tf_op jit(solution)/shard_map/factor/pallas_call | solution.py:165
  115.0 1.2 mine.1
  116.2 0.0 collective-permute-done.1.total_ref
  116.2 2.9 %finish.1 = (f32[32,14336]{1,0:T(8,128)}, bf16[1,64,14336]{2,1,0:T(8,128)(2,1)}) custom-call(s32[2]{0:T(128)S(1)} %get-tuple-element.9.sides_ref, f32[16,15,8,128]{3,2,1,0:T(8,128)S(1)} %collective-permute-done.1.total_ref, bf16[32,128]{1,0:T(8,128)(2,1)S(1)} %get-tuple-element.12.inverse_ref, bf16[64,128]{1,0:T(8,128)(2,1)S(1)} %get-tuple-element.13.basis_ref, ...), custom_call_target="tpu_custom_call" | custom-call | tf_op jit(solution)/shard_map/finish/pallas_call | solution.py:243
  (7 shorter events, 0.0 us)
Async XLA Ops:
  30.1 7.0 %collective-permute-start = (f32[16,15,8,128]{3,2,1,0:T(8,128)S(1)}, f32[16,15,8,128]{3,2,1,0:T(8,128)S(1)}, u32[]{:S(2)}, u32[]{:S(2)}) collective-permute-start(f32[16,15,8,128]{3,2,1,0:T(8,128)S(1)} %term.3), channel_id=1, source_target_pairs={{0,12},{12,0},{1,13},{13,1},{2,14},{14,2},{3,15},{15,3},{4,16},{16... | collective-permute-start | bytes 2949128 | tf_op jit(solution)/shard_map/ppermute | solution.py:276
  104.7 11.5 %collective-permute-start.1 = (f32[16,15,8,128]{3,2,1,0:T(8,128)S(1)}, f32[16,15,8,128]{3,2,1,0:T(8,128)S(1)}, u32[]{:S(2)}, u32[]{:S(2)}) collective-permute-start(f32[16,15,8,128]{3,2,1,0:T(8,128)S(1)} %all_to_all.35.total_ref), channel_id=1, source_target_pairs={{0,12},{12,0},{1,13},{13,1},{2,14},{14,2},{3,15},{15,3},{4,16},{16... | collective-permute-start | bytes 2949128 | tf_op jit(solution)/shard_map/ppermute | solution.py:286

commit v7 on v6

--- a/solution.py
+++ b/solution.py
@@ -13,7 +13,6 @@
 NP = PAIR * PAIR
 SUB, LANE = 8, 128
 RANK = 32
-TILES = 4
 COPIES = 2
 AHEAD = 4
 VMEM = 24 * 1024 * 1024
@@ -277,12 +276,9 @@
     part = term(0, sides, shares, grads) + away
     used = part.shape[1]
     part = jnp.sum(exchange(part, ("x", "near", "side")), axis=0)
-    part = jnp.pad(part, ((0, NY * TILES - used), (0, 0), (0, 0)))
-    part = jnp.sum(exchange(part.reshape(NY, TILES, SUB, LANE), "y"), axis=0)
+    part = jnp.sum(spread(part, "y"), axis=0)
     part = jnp.sum(spread(part, "far"), axis=0)
-
-    total = spread(part, "y").reshape(NY * TILES, SUB, LANE)[:used]
-    total = spread(total, ("x", "near", "side"))
+    total = spread(part, ("x", "near", "side"))
     away = lax.ppermute(total, "c", swap)
     inverse, basis = factor(total[0, used - 1], shares, grads.shape[1])
     done = mine(sides, total, inverse, basis, grads, groups)

time: 119 us -> 117 us (0.983)
  starting transfers between devices: 13.7 us -> 12.2 us
    ppermute x1, starting transfers between devices: 8.89 us -> 7.38 us  [per_device(): away = lax.ppermute(total, 'c', swap)]
    all_to_all x6 -> x5, blocking collectives: 92.9 us -> 92.2 us  [exchange(): return lax.all_to_all(blocks, axis, 0, 0, tiled=True)]
where the time goes in v7:
time: 117 us
  blocking collectives  92.2 us (79%)
  starting transfers between devices  12.2 us (10%)
  Pallas kernels  10.4 us (9%)
    all_to_all x5, blocking collectives, exchange(): return lax.all_to_all(blocks, axis, 0, 0, tiled=True)  92.2 us
    ppermute x1, starting transfers between devices, per_device(): away = lax.ppermute(total, 'c', swap)  7.38 us
    ppermute x1, starting transfers between devices, per_device(): away = lax.ppermute(term(1, sides, shares, grads), 'c', swap)  4.81 us
    pallas_call x1, Pallas kernels, finish(): pl.pallas_call(functools.partial(finish_kernel, groups), in_specs=[pl.Blo...  2.89 us
    pallas_call x1, Pallas kernels, project(): pl.pallas_call(project_kernel, in_specs=[pl.BlockSpec(memory_space=pltpu....  2.78 us
  transfers between devices with their start and end apart: 2, of which 1 were waited for; matrix products, arithmetic and copies ran while one was open for 0% of the time, Pallas kernels for 3%

profile of v7, /device:TPU:1, one launch (start us, length us, event | category | flops | bytes accessed | tf_op | source)
XLA Modules:
  0.0 116.9 jit_solution(13036325558369076307)
XLA Ops:
  0.6 2.8 %project.1 = (f32[12,16,128]{2,1,0:T(8,128)S(1)}, bf16[1,64,14336]{2,1,0:T(8,128)(2,1)S(1)}, s32[2]{0:T(128)S(1)}) custom-call(s32[1]{0:T(128)} %bitcast.own_ref, bf16[1,64,14336]{2,1,0:T(8,128)(2,1)} %grads_ref.1, f32[32,14336]{1,0:T(8,128)} %q_ref.1), custom_call_target="tpu_custom_call" | custom-call | tf_op jit(solution)/shard_map/project/pallas_call | solution.py:75
  3.4 25.5 %all_to_all.25.shares_ref = f32[12,16,128]{2,1,0:T(8,128)S(1)} all-to-all(f32[12,16,128]{2,1,0:T(8,128)S(1)} %get-tuple-element.10), channel_id=1, replica_groups=mesh['y'=4,'side'=2,'x'=4,'c'=2,'far'=6,'near'=2] {'far','near'}, dimensions={0} | all-to-all | bytes 196608 | tf_op jit(solution)/shard_map/all_to_all | solution.py:261
  28.9 1.1 term.3
  30.1 4.8 %collective-permute-start = (f32[16,15,8,128]{3,2,1,0:T(8,128)S(1)}, f32[16,15,8,128]{3,2,1,0:T(8,128)S(1)}, u32[]{:S(2)}, u32[]{:S(2)}) collective-permute-start(f32[16,15,8,128]{3,2,1,0:T(8,128)S(1)} %term.3), channel_id=1, source_target_pairs={{0,12},{12,0},{1,13},{13,1},{2,14},{14,2},{3,15},{15,3},{4,16},{16... | collective-permute-start | bytes 2949128 | tf_op jit(solution)/shard_map/ppermute | solution.py:275
  34.9 1.1 term.2
  36.0 1.1 collective-permute-done
  37.0 0.1 add.3
  37.2 19.0 %all_to_all.26 = f32[16,15,8,128]{3,2,1,0:T(8,128)S(1)} all-to-all(f32[16,15,8,128]{3,2,1,0:T(8,128)S(1)} %add.3), channel_id=1, replica_groups=mesh['y'=4,'side'=2,'x'=4,'c'=2,'far'=6,'near'=2] {'x','near','side'}, dimensions={0} | all-to-all | bytes 1966080 | tf_op jit(solution)/shard_map/all_to_all | solution.py:261
  56.1 0.1 reduce_sum.27
  56.2 14.6 %all_to_all.27 = f32[4,15,8,128]{3,2,1,0:T(8,128)S(1)} all-to-all(f32[4,15,8,128]{3,2,1,0:T(8,128)S(1)} %broadcast_in_dim.6), channel_id=1, replica_groups=mesh['y'=4,'side'=2,'x'=4,'c'=2,'far'=6,'near'=2] {'y'}, dimensions={0} | all-to-all | bytes 491520 | tf_op jit(solution)/shard_map/all_to_all | solution.py:261
  70.8 15.8 %all_to_all.28 = f32[6,15,8,128]{3,2,1,0:T(8,128)S(1)} all-to-all(f32[6,15,8,128]{3,2,1,0:T(8,128)S(1)} %broadcast_in_dim.7), channel_id=1, replica_groups=mesh['y'=4,'side'=2,'x'=4,'c'=2,'far'=6,'near'=2] {'far'}, dimensions={0} | all-to-all | bytes 737280 | tf_op jit(solution)/shard_map/all_to_all | solution.py:261
  86.7 0.1 broadcast_in_dim.8
  86.7 17.3 %all_to_all.29.total_ref = f32[16,15,8,128]{3,2,1,0:T(8,128)S(1)} all-to-all(f32[16,15,8,128]{3,2,1,0:T(8,128)S(1)} %broadcast_in_dim.8), channel_id=1, replica_groups=mesh['y'=4,'side'=2,'x'=4,'c'=2,'far'=6,'near'=2] {'x','near','side'}, dimensions={0} | all-to-all | bytes 1966080 | tf_op jit(solution)/shard_map/all_to_all | solution.py:261
  104.0 7.4 %collective-permute-start.1 = (f32[16,15,8,128]{3,2,1,0:T(8,128)S(1)}, f32[16,15,8,128]{3,2,1,0:T(8,128)S(1)}, u32[]{:S(2)}, u32[]{:S(2)}) collective-permute-start(f32[16,15,8,128]{3,2,1,0:T(8,128)S(1)} %all_to_all.29.total_ref), channel_id=1, source_target_pairs={{0,12},{12,0},{1,13},{13,1},{2,14},{14,2},{3,15},{15,3},{4,16},{16... | collective-permute-start | bytes 2949128 | tf_op jit(solution)/shard_map/ppermute | solution.py:282
  111.4 1.4 %factor.1 = (bf16[32,128]{1,0:T(8,128)(2,1)S(1)}, bf16[64,128]{1,0:T(8,128)(2,1)S(1)}) custom-call(f32[8,128]{1,0:T(8,128)S(1)} %slice_bitcast_fusion.gram_ref, f32[12,16,128]{2,1,0:T(8,128)S(1)} %all_to_all.25.shares_ref), custom_call_target="tpu_custom_call" | custom-call | flops 4194304 | bytes 1048576 | tf_op jit(solution)/shard_map/factor/pallas_call | solution.py:164
  112.8 1.2 %mine.1 = (f32[32,7168]{1,0:T(8,128)S(1)}, bf16[1,64,7168]{2,1,0:T(8,128)(2,1)S(1)}) custom-call(s32[2]{0:T(128)S(1)} %get-tuple-element.9.sides_ref, f32[16,15,8,128]{3,2,1,0:T(8,128)S(1)} %all_to_all.29.total_ref, bf16[32,128]{1,0:T(8,128)(2,1)S(1)} %get-tuple-element.12.inverse_ref, bf16[64,128]{1,0:T(8,128)(2,1)S(1)} %get-tuple-element.13.basis_ref, ...), custom_call_target="tpu_custom_call" | custom-call | flops 146800640 | bytes 2752512 | tf_op jit(solution)/shard_map/mine/pallas_call | solution.py:205
  114.0 0.0 collective-permute-done.1.total_ref
  114.0 2.9 %finish.1 = (f32[32,14336]{1,0:T(8,128)}, bf16[1,64,14336]{2,1,0:T(8,128)(2,1)}) custom-call(s32[2]{0:T(128)S(1)} %get-tuple-element.9.sides_ref, f32[16,15,8,128]{3,2,1,0:T(8,128)S(1)} %collective-permute-done.1.total_ref, bf16[32,128]{1,0:T(8,128)(2,1)S(1)} %get-tuple-element.12.inverse_ref, bf16[64,128]{1,0:T(8,128)(2,1)S(1)} %get-tuple-element.13.basis_ref, ...), custom_call_target="tpu_custom_call" | custom-call | tf_op jit(solution)/shard_map/finish/pallas_call | solution.py:242
  (5 shorter events, 0.1 us)
Async XLA Ops:
  30.1 7.0 %collective-permute-start = (f32[16,15,8,128]{3,2,1,0:T(8,128)S(1)}, f32[16,15,8,128]{3,2,1,0:T(8,128)S(1)}, u32[]{:S(2)}, u32[]{:S(2)}) collective-permute-start(f32[16,15,8,128]{3,2,1,0:T(8,128)S(1)} %term.3), channel_id=1, source_target_pairs={{0,12},{12,0},{1,13},{13,1},{2,14},{14,2},{3,15},{15,3},{4,16},{16... | collective-permute-start | bytes 2949128 | tf_op jit(solution)/shard_map/ppermute | solution.py:275
  104.0 10.0 %collective-permute-start.1 = (f32[16,15,8,128]{3,2,1,0:T(8,128)S(1)}, f32[16,15,8,128]{3,2,1,0:T(8,128)S(1)}, u32[]{:S(2)}, u32[]{:S(2)}) collective-permute-start(f32[16,15,8,128]{3,2,1,0:T(8,128)S(1)} %all_to_all.29.total_ref), channel_id=1, source_target_pairs={{0,12},{12,0},{1,13},{13,1},{2,14},{14,2},{3,15},{15,3},{4,16},{16... | collective-permute-start | bytes 2949128 | tf_op jit(solution)/shard_map/ppermute | solution.py:282

commit v8 on v7

--- a/solution.py
+++ b/solution.py
@@ -101,7 +101,7 @@
     part = dot(stack, grads_ref[0, :, half_of(side, sides_ref, half)], (1, 0))
     part = part[:RANK] + part[RANK:]
     tiles = out_ref.shape[1] - 1
-    wide = dot(left, jnp.concatenate([left] * NX, axis=0), (1, 1), HIGH) / shares_ref.shape[0]
+    wide = dot(left, jnp.concatenate([left] * NX, axis=0), (1, 1), HIGH) / PAIR
     slot = lax.broadcasted_iota(jnp.int32, (SUB, LANE), 1) // RANK
     tile = jnp.zeros((SUB, LANE), F32)
     for x in range(NX):
@@ -174,7 +174,7 @@
 
 
 def solve(total_ref, inverse_ref, groups):
-    tiles = total_ref.shape[1] - 1
+    tiles = total_ref.shape[1]
     columns = []
     for t in range(NP * tiles):
         parts = [total_ref[x * NP + t // tiles, t % tiles] for x in range(NX)]
@@ -274,13 +274,13 @@
     shares = exchange(shares, ("far", "near"))
     away = lax.ppermute(term(1, sides, shares, grads), "c", swap)
     part = term(0, sides, shares, grads) + away
-    used = part.shape[1]
     part = jnp.sum(exchange(part, ("x", "near", "side")), axis=0)
     part = jnp.sum(spread(part, "y"), axis=0)
-    part = jnp.sum(spread(part, "far"), axis=0)
+    gram = part[-1]
+    part = jnp.sum(spread(part[:-1], "far"), axis=0)
     total = spread(part, ("x", "near", "side"))
     away = lax.ppermute(total, "c", swap)
-    inverse, basis = factor(total[0, used - 1], shares, grads.shape[1])
+    inverse, basis = factor(gram, shares, grads.shape[1])
     done = mine(sides, total, inverse, basis, grads, groups)
     return tuple(finish(sides, away, inverse, basis, grads, groups, done))
 

time: 117 us -> 116 us (level)
  blocking collectives: 92.2 us -> 90.3 us
    all_to_all x5, blocking collectives: 92.2 us -> 90.3 us  [exchange(): return lax.all_to_all(blocks, axis, 0, 0, tiled=True)]
where the time goes in v8:
time: 116 us; the launch traced here: 115 us
  blocking collectives  90.3 us (78%)
  starting transfers between devices  12.1 us (10%)
  Pallas kernels  10.4 us (9%)
    all_to_all x5, blocking collectives, exchange(): return lax.all_to_all(blocks, axis, 0, 0, tiled=True)  90.3 us
    ppermute x1, starting transfers between devices, per_device(): away = lax.ppermute(total, 'c', swap)  7.28 us
    ppermute x1, starting transfers between devices, per_device(): away = lax.ppermute(term(1, sides, shares, grads), 'c', swap)  4.81 us
    pallas_call x1, Pallas kernels, finish(): pl.pallas_call(functools.partial(finish_kernel, groups), in_specs=[pl.Blo...  2.89 us
    pallas_call x1, Pallas kernels, project(): pl.pallas_call(project_kernel, in_specs=[pl.BlockSpec(memory_space=pltpu....  2.78 us
  transfers between devices with their start and end apart: 2, of which 1 were waited for; matrix products, arithmetic and copies ran while one was open for 0% of the time, Pallas kernels for 3%

profile of v8, /device:TPU:1, one launch (start us, length us, event | category | flops | bytes accessed | tf_op | source)
XLA Modules:
  0.0 114.9 jit_solution(5267938074600697619)
XLA Ops:
  0.6 2.8 %project.1 = (f32[12,16,128]{2,1,0:T(8,128)S(1)}, bf16[1,64,14336]{2,1,0:T(8,128)(2,1)S(1)}, s32[2]{0:T(128)S(1)}) custom-call(s32[1]{0:T(128)} %bitcast.own_ref, bf16[1,64,14336]{2,1,0:T(8,128)(2,1)} %grads_ref.1, f32[32,14336]{1,0:T(8,128)} %q_ref.1), custom_call_target="tpu_custom_call" | custom-call | tf_op jit(solution)/shard_map/project/pallas_call | solution.py:75
  3.4 25.5 %all_to_all.25.shares_ref = f32[12,16,128]{2,1,0:T(8,128)S(1)} all-to-all(f32[12,16,128]{2,1,0:T(8,128)S(1)} %get-tuple-element.10), channel_id=1, replica_groups=mesh['y'=4,'side'=2,'x'=4,'c'=2,'far'=6,'near'=2] {'far','near'}, dimensions={0} | all-to-all | bytes 196608 | tf_op jit(solution)/shard_map/all_to_all | solution.py:261
  28.9 1.1 term.3
  30.1 4.8 %collective-permute-start = (f32[16,15,8,128]{3,2,1,0:T(8,128)S(1)}, f32[16,15,8,128]{3,2,1,0:T(8,128)S(1)}, u32[]{:S(2)}, u32[]{:S(2)}) collective-permute-start(f32[16,15,8,128]{3,2,1,0:T(8,128)S(1)} %term.3), channel_id=1, source_target_pairs={{0,12},{12,0},{1,13},{13,1},{2,14},{14,2},{3,15},{15,3},{4,16},{16... | collective-permute-start | bytes 2949128 | tf_op jit(solution)/shard_map/ppermute | solution.py:275
  34.9 1.1 term.2
  36.0 1.1 collective-permute-done
  37.0 0.1 add.3
  37.2 19.0 %all_to_all.26 = f32[16,15,8,128]{3,2,1,0:T(8,128)S(1)} all-to-all(f32[16,15,8,128]{3,2,1,0:T(8,128)S(1)} %add.3), channel_id=1, replica_groups=mesh['y'=4,'side'=2,'x'=4,'c'=2,'far'=6,'near'=2] {'x','near','side'}, dimensions={0} | all-to-all | bytes 1966080 | tf_op jit(solution)/shard_map/all_to_all | solution.py:261
  56.1 0.1 reduce_sum.27
  56.2 14.6 %all_to_all.27 = f32[4,15,8,128]{3,2,1,0:T(8,128)S(1)} all-to-all(f32[4,15,8,128]{3,2,1,0:T(8,128)S(1)} %broadcast_in_dim.6), channel_id=1, replica_groups=mesh['y'=4,'side'=2,'x'=4,'c'=2,'far'=6,'near'=2] {'y'}, dimensions={0} | all-to-all | bytes 491520 | tf_op jit(solution)/shard_map/all_to_all | solution.py:261
  70.8 15.6 %all_to_all.28 = f32[6,14,8,128]{3,2,1,0:T(8,128)S(1)} all-to-all(f32[6,14,8,128]{3,2,1,0:T(8,128)S(1)} %broadcast_in_dim.7), channel_id=1, replica_groups=mesh['y'=4,'side'=2,'x'=4,'c'=2,'far'=6,'near'=2] {'far'}, dimensions={0} | all-to-all | bytes 688128 | tf_op jit(solution)/shard_map/all_to_all | solution.py:261
  86.5 0.1 broadcast_in_dim.8
  86.6 15.6 %all_to_all.29.total_ref = f32[16,14,8,128]{3,2,1,0:T(8,128)S(1)} all-to-all(f32[16,14,8,128]{3,2,1,0:T(8,128)S(1)} %broadcast_in_dim.8), channel_id=1, replica_groups=mesh['y'=4,'side'=2,'x'=4,'c'=2,'far'=6,'near'=2] {'x','near','side'}, dimensions={0} | all-to-all | bytes 1835008 | tf_op jit(solution)/shard_map/all_to_all | solution.py:261
  102.1 7.3 %collective-permute-start.1 = (f32[16,14,8,128]{3,2,1,0:T(8,128)S(1)}, f32[16,14,8,128]{3,2,1,0:T(8,128)S(1)}, u32[]{:S(2)}, u32[]{:S(2)}) collective-permute-start(f32[16,14,8,128]{3,2,1,0:T(8,128)S(1)} %all_to_all.29.total_ref), channel_id=1, source_target_pairs={{0,12},{12,0},{1,13},{13,1},{2,14},{14,2},{3,15},{15,3},{4,16},{16... | collective-permute-start | bytes 2752520 | tf_op jit(solution)/shard_map/ppermute | solution.py:282
  109.4 1.4 %factor.1 = (bf16[32,128]{1,0:T(8,128)(2,1)S(1)}, bf16[64,128]{1,0:T(8,128)(2,1)S(1)}) custom-call(f32[8,128]{1,0:T(8,128)S(1)} %slice_bitcast_fusion.gram_ref, f32[12,16,128]{2,1,0:T(8,128)S(1)} %all_to_all.25.shares_ref), custom_call_target="tpu_custom_call" | custom-call | flops 4194304 | bytes 1048576 | tf_op jit(solution)/shard_map/factor/pallas_call | solution.py:164
  110.8 1.2 %mine.1 = (f32[32,7168]{1,0:T(8,128)S(1)}, bf16[1,64,7168]{2,1,0:T(8,128)(2,1)S(1)}) custom-call(s32[2]{0:T(128)S(1)} %get-tuple-element.9.sides_ref, f32[16,14,8,128]{3,2,1,0:T(8,128)S(1)} %all_to_all.29.total_ref, bf16[32,128]{1,0:T(8,128)(2,1)S(1)} %get-tuple-element.12.inverse_ref, bf16[64,128]{1,0:T(8,128)(2,1)S(1)} %get-tuple-element.13.basis_ref, ...), custom_call_target="tpu_custom_call" | custom-call | flops 146800640 | bytes 2752512 | tf_op jit(solution)/shard_map/mine/pallas_call | solution.py:205
  112.0 0.0 collective-permute-done.1.total_ref
  112.0 2.9 %finish.1 = (f32[32,14336]{1,0:T(8,128)}, bf16[1,64,14336]{2,1,0:T(8,128)(2,1)}) custom-call(s32[2]{0:T(128)S(1)} %get-tuple-element.9.sides_ref, f32[16,14,8,128]{3,2,1,0:T(8,128)S(1)} %collective-permute-done.1.total_ref, bf16[32,128]{1,0:T(8,128)(2,1)S(1)} %get-tuple-element.12.inverse_ref, bf16[64,128]{1,0:T(8,128)(2,1)S(1)} %get-tuple-element.13.basis_ref, ...), custom_call_target="tpu_custom_call" | custom-call | tf_op jit(solution)/shard_map/finish/pallas_call | solution.py:242
  (6 shorter events, 0.1 us)
Async XLA Ops:
  30.1 7.0 %collective-permute-start = (f32[16,15,8,128]{3,2,1,0:T(8,128)S(1)}, f32[16,15,8,128]{3,2,1,0:T(8,128)S(1)}, u32[]{:S(2)}, u32[]{:S(2)}) collective-permute-start(f32[16,15,8,128]{3,2,1,0:T(8,128)S(1)} %term.3), channel_id=1, source_target_pairs={{0,12},{12,0},{1,13},{13,1},{2,14},{14,2},{3,15},{15,3},{4,16},{16... | collective-permute-start | bytes 2949128 | tf_op jit(solution)/shard_map/ppermute | solution.py:275
  102.1 9.9 %collective-permute-start.1 = (f32[16,14,8,128]{3,2,1,0:T(8,128)S(1)}, f32[16,14,8,128]{3,2,1,0:T(8,128)S(1)}, u32[]{:S(2)}, u32[]{:S(2)}) collective-permute-start(f32[16,14,8,128]{3,2,1,0:T(8,128)S(1)} %all_to_all.29.total_ref), channel_id=1, source_target_pairs={{0,12},{12,0},{1,13},{13,1},{2,14},{14,2},{3,15},{15,3},{4,16},{16... | collective-permute-start | bytes 2752520 | tf_op jit(solution)/shard_map/ppermute | solution.py:282

commit v9 on v8

--- a/solution.py
+++ b/solution.py
@@ -193,10 +193,14 @@
     return pl.ds(pl.multiple_of(sides_ref[side] * half, LANE), half)
 
 
-def mine_kernel(groups, sides_ref, total_ref, inverse_ref, basis_ref, grads_ref, q_ref, resid_ref):
+def mine_kernel(groups, sides_ref, total_ref, inverse_ref, basis_ref, grads_ref, q_ref, resid_ref, q_buf, sem):
+    here = half_of(0, sides_ref, q_buf.shape[1])
     q_new = solve(total_ref, inverse_ref, groups)
-    q_ref[...] = q_new
-    resid_ref[0] = residual(q_new, basis_ref, grads_ref[0, :, half_of(0, sides_ref, q_ref.shape[1])])
+    q_buf[...] = q_new
+    copy = pltpu.make_async_copy(q_buf, q_ref.at[:, here], sem)
+    copy.start()
+    resid_ref[0] = residual(q_new, basis_ref, grads_ref[0, :, here])
+    copy.wait()
 
 
 def mine(sides, total, inverse, basis, grads, groups):
@@ -205,8 +209,9 @@
     return pl.pallas_call(
         functools.partial(mine_kernel, groups),
         in_specs=[pl.BlockSpec(memory_space=pltpu.SMEM)] + [pl.BlockSpec(memory_space=pltpu.VMEM)] * 4,
-        out_specs=(pl.BlockSpec(memory_space=pltpu.VMEM),) * 2,
-        out_shape=(pltpu.VMEM((RANK, half), F32), pltpu.VMEM((1, rows, half), BF16)),
+        out_specs=(pl.BlockSpec(memory_space=pl.ANY), pl.BlockSpec(memory_space=pltpu.VMEM)),
+        out_shape=(pltpu.HBM((RANK, cols), F32), pltpu.VMEM((1, rows, half), BF16)),
+        scratch_shapes=[pltpu.VMEM((RANK, half), F32), pltpu.SemaphoreType.DMA],
         compiler_params=pltpu.CompilerParams(vmem_limit_bytes=VMEM),
         cost_estimate=pl.CostEstimate(flops=2 * 160 * rows * half, bytes_accessed=6 * rows * half, transcendentals=0),
         name="mine",
@@ -220,18 +225,16 @@
     half = q_buf.shape[1]
     here, there = half_of(0, sides_ref, half), half_of(1, sides_ref, half)
     copies = [
-        pltpu.make_async_copy(mine_q_ref, q_ref.at[:, here], sems.at[0]),
-        pltpu.make_async_copy(mine_resid_ref, resid_ref.at[:, :, here], sems.at[1]),
-        pltpu.make_async_copy(q_buf, q_ref.at[:, there], sems.at[2]),
-        pltpu.make_async_copy(resid_buf, resid_ref.at[:, :, there], sems.at[3]),
+        pltpu.make_async_copy(mine_resid_ref, resid_ref.at[:, :, here], sems.at[0]),
+        pltpu.make_async_copy(q_buf, q_ref.at[:, there], sems.at[1]),
+        pltpu.make_async_copy(resid_buf, resid_ref.at[:, :, there], sems.at[2]),
     ]
     copies[0].start()
-    copies[1].start()
     q_new = solve(total_ref, inverse_ref, groups)
     q_buf[...] = q_new
+    copies[1].start()
+    resid_buf[0] = residual(q_new, basis_ref, grads_ref[0, :, there])
     copies[2].start()
-    resid_buf[0] = residual(q_new, basis_ref, grads_ref[0, :, there])
-    copies[3].start()
     for copy in copies:
         copy.wait()
 
@@ -241,7 +244,8 @@
     half = cols // NC
     return pl.pallas_call(
         functools.partial(finish_kernel, groups),
-        in_specs=[pl.BlockSpec(memory_space=pltpu.SMEM)] + [pl.BlockSpec(memory_space=pltpu.VMEM)] * 6,
+        in_specs=[pl.BlockSpec(memory_space=pltpu.SMEM)] + [pl.BlockSpec(memory_space=pltpu.VMEM)] * 4
+        + [pl.BlockSpec(memory_space=pl.ANY), pl.BlockSpec(memory_space=pltpu.VMEM)],
         out_specs=(pl.BlockSpec(memory_space=pl.ANY),) * 2,
         out_shape=(
             jax.ShapeDtypeStruct((RANK, cols), F32),
@@ -250,8 +254,9 @@
         scratch_shapes=[
             pltpu.VMEM((RANK, half), F32),
             pltpu.VMEM((1, rows, half), BF16),
-            pltpu.SemaphoreType.DMA((4,)),
+            pltpu.SemaphoreType.DMA((3,)),
         ],
+        input_output_aliases={5: 0},
         compiler_params=pltpu.CompilerParams(vmem_limit_bytes=VMEM),
         name="finish",
     )(sides, total, inverse, basis, grads, *done)

time: 116 us -> 116 us (level)
  transfers between devices with their start and end apart: 2 -> 2, of which waited for: 1 -> 1; matrix products, arithmetic and copies ran while one was open for 0% -> 0% of each run, Pallas kernels for 3% -> 4%
where the time goes in v9:
time: 116 us; the launch traced here: 115 us
  blocking collectives  90.3 us (78%)
  starting transfers between devices  12.1 us (10%)
  Pallas kernels  10.9 us (9%)
    all_to_all x5, blocking collectives, exchange(): return lax.all_to_all(blocks, axis, 0, 0, tiled=True)  90.3 us
    ppermute x1, starting transfers between devices, per_device(): away = lax.ppermute(total, 'c', swap)  7.28 us
    ppermute x1, starting transfers between devices, per_device(): away = lax.ppermute(term(1, sides, shares, grads), 'c', swap)  4.81 us
    pallas_call x1, Pallas kernels, project(): pl.pallas_call(project_kernel, in_specs=[pl.BlockSpec(memory_space=pltpu....  2.78 us
    pallas_call x1, Pallas kernels, finish(): pl.pallas_call(functools.partial(finish_kernel, groups), in_specs=[pl.Blo...  2.58 us
  transfers between devices with their start and end apart: 2, of which 1 were waited for; matrix products, arithmetic and copies ran while one was open for 0% of the time, Pallas kernels for 4%

profile of v9, /device:TPU:1, one launch (start us, length us, event | category | flops | bytes accessed | tf_op | source)
XLA Modules:
  0.0 115.4 jit_solution(9512061653214046382)
XLA Ops:
  0.6 2.8 %project.1 = (f32[12,16,128]{2,1,0:T(8,128)S(1)}, bf16[1,64,14336]{2,1,0:T(8,128)(2,1)S(1)}, s32[2]{0:T(128)S(1)}) custom-call(s32[1]{0:T(128)} %bitcast.own_ref, bf16[1,64,14336]{2,1,0:T(8,128)(2,1)} %grads_ref.1, f32[32,14336]{1,0:T(8,128)} %q_ref.1), custom_call_target="tpu_custom_call" | custom-call | tf_op jit(solution)/shard_map/project/pallas_call | solution.py:75
  3.4 25.5 %all_to_all.25.shares_ref = f32[12,16,128]{2,1,0:T(8,128)S(1)} all-to-all(f32[12,16,128]{2,1,0:T(8,128)S(1)} %get-tuple-element.10), channel_id=1, replica_groups=mesh['y'=4,'side'=2,'x'=4,'c'=2,'far'=6,'near'=2] {'far','near'}, dimensions={0} | all-to-all | bytes 196608 | tf_op jit(solution)/shard_map/all_to_all | solution.py:266
  28.9 1.1 term.3
  30.1 4.8 %collective-permute-start = (f32[16,15,8,128]{3,2,1,0:T(8,128)S(1)}, f32[16,15,8,128]{3,2,1,0:T(8,128)S(1)}, u32[]{:S(2)}, u32[]{:S(2)}) collective-permute-start(f32[16,15,8,128]{3,2,1,0:T(8,128)S(1)} %term.3), channel_id=1, source_target_pairs={{0,12},{12,0},{1,13},{13,1},{2,14},{14,2},{3,15},{15,3},{4,16},{16... | collective-permute-start | bytes 2949128 | tf_op jit(solution)/shard_map/ppermute | solution.py:280
  34.9 1.1 term.2
  36.0 1.1 collective-permute-done
  37.0 0.1 add.3
  37.2 19.0 %all_to_all.26 = f32[16,15,8,128]{3,2,1,0:T(8,128)S(1)} all-to-all(f32[16,15,8,128]{3,2,1,0:T(8,128)S(1)} %add.3), channel_id=1, replica_groups=mesh['y'=4,'side'=2,'x'=4,'c'=2,'far'=6,'near'=2] {'x','near','side'}, dimensions={0} | all-to-all | bytes 1966080 | tf_op jit(solution)/shard_map/all_to_all | solution.py:266
  56.1 0.1 reduce_sum.27
  56.2 14.6 %all_to_all.27 = f32[4,15,8,128]{3,2,1,0:T(8,128)S(1)} all-to-all(f32[4,15,8,128]{3,2,1,0:T(8,128)S(1)} %broadcast_in_dim.6), channel_id=1, replica_groups=mesh['y'=4,'side'=2,'x'=4,'c'=2,'far'=6,'near'=2] {'y'}, dimensions={0} | all-to-all | bytes 491520 | tf_op jit(solution)/shard_map/all_to_all | solution.py:266
  70.8 15.6 %all_to_all.28 = f32[6,14,8,128]{3,2,1,0:T(8,128)S(1)} all-to-all(f32[6,14,8,128]{3,2,1,0:T(8,128)S(1)} %broadcast_in_dim.7), channel_id=1, replica_groups=mesh['y'=4,'side'=2,'x'=4,'c'=2,'far'=6,'near'=2] {'far'}, dimensions={0} | all-to-all | bytes 688128 | tf_op jit(solution)/shard_map/all_to_all | solution.py:266
  86.5 0.1 broadcast_in_dim.8
  86.6 15.6 %all_to_all.29.total_ref = f32[16,14,8,128]{3,2,1,0:T(8,128)S(1)} all-to-all(f32[16,14,8,128]{3,2,1,0:T(8,128)S(1)} %broadcast_in_dim.8), channel_id=1, replica_groups=mesh['y'=4,'side'=2,'x'=4,'c'=2,'far'=6,'near'=2] {'x','near','side'}, dimensions={0} | all-to-all | bytes 1835008 | tf_op jit(solution)/shard_map/all_to_all | solution.py:266
  102.1 7.3 %collective-permute-start.1 = (f32[16,14,8,128]{3,2,1,0:T(8,128)S(1)}, f32[16,14,8,128]{3,2,1,0:T(8,128)S(1)}, u32[]{:S(2)}, u32[]{:S(2)}) collective-permute-start(f32[16,14,8,128]{3,2,1,0:T(8,128)S(1)} %all_to_all.29.total_ref), channel_id=1, source_target_pairs={{0,12},{12,0},{1,13},{13,1},{2,14},{14,2},{3,15},{15,3},{4,16},{16... | collective-permute-start | bytes 2752520 | tf_op jit(solution)/shard_map/ppermute | solution.py:287
  109.4 1.4 %factor.1 = (bf16[32,128]{1,0:T(8,128)(2,1)S(1)}, bf16[64,128]{1,0:T(8,128)(2,1)S(1)}) custom-call(f32[8,128]{1,0:T(8,128)S(1)} %slice_bitcast_fusion.gram_ref, f32[12,16,128]{2,1,0:T(8,128)S(1)} %all_to_all.25.shares_ref), custom_call_target="tpu_custom_call" | custom-call | flops 4194304 | bytes 1048576 | tf_op jit(solution)/shard_map/factor/pallas_call | solution.py:164
  110.8 2.0 %mine.1 = (f32[32,14336]{1,0:T(8,128)}, bf16[1,64,7168]{2,1,0:T(8,128)(2,1)S(1)}) custom-call(s32[2]{0:T(128)S(1)} %get-tuple-element.9.sides_ref, f32[16,14,8,128]{3,2,1,0:T(8,128)S(1)} %all_to_all.29.total_ref, bf16[32,128]{1,0:T(8,128)(2,1)S(1)} %get-tuple-element.12.inverse_ref, bf16[64,128]{1,0:T(8,128)(2,1)S(1)} %get-tuple-element.13.basis_ref, ...), custom_call_target="tpu_custom_call" | custom-call | flops 146800640 | bytes 2752512 | tf_op jit(solution)/shard_map/mine/pallas_call | solution.py:209
  112.8 0.0 collective-permute-done.1.total_ref
  112.8 2.6 %finish.1 = (f32[32,14336]{1,0:T(8,128)}, bf16[1,64,14336]{2,1,0:T(8,128)(2,1)}) custom-call(s32[2]{0:T(128)S(1)} %get-tuple-element.9.sides_ref, f32[16,14,8,128]{3,2,1,0:T(8,128)S(1)} %collective-permute-done.1.total_ref, bf16[32,128]{1,0:T(8,128)(2,1)S(1)} %get-tuple-element.12.inverse_ref, ...), custom_call_target="tpu_custom_call", output_to_operand_aliasing={{0}: (5, {})} | custom-call | tf_op jit(solution)/shard_map/finish/pallas_call | solution.py:245
  (6 shorter events, 0.1 us)
Async XLA Ops:
  30.1 7.0 %collective-permute-start = (f32[16,15,8,128]{3,2,1,0:T(8,128)S(1)}, f32[16,15,8,128]{3,2,1,0:T(8,128)S(1)}, u32[]{:S(2)}, u32[]{:S(2)}) collective-permute-start(f32[16,15,8,128]{3,2,1,0:T(8,128)S(1)} %term.3), channel_id=1, source_target_pairs={{0,12},{12,0},{1,13},{13,1},{2,14},{14,2},{3,15},{15,3},{4,16},{16... | collective-permute-start | bytes 2949128 | tf_op jit(solution)/shard_map/ppermute | solution.py:280
  102.1 10.7 %collective-permute-start.1 = (f32[16,14,8,128]{3,2,1,0:T(8,128)S(1)}, f32[16,14,8,128]{3,2,1,0:T(8,128)S(1)}, u32[]{:S(2)}, u32[]{:S(2)}) collective-permute-start(f32[16,14,8,128]{3,2,1,0:T(8,128)S(1)} %all_to_all.29.total_ref), channel_id=1, source_target_pairs={{0,12},{12,0},{1,13},{13,1},{2,14},{14,2},{3,15},{15,3},{4,16},{16... | collective-permute-start | bytes 2752520 | tf_op jit(solution)/shard_map/ppermute | solution.py:287
